TPU v7x, 1024 devices: a whole 4x8x16 slice. The times are simulated.
1024 devices in a mesh: side: 2 (over x_hi), grp: 32 (over z, core), shard: 16 (over x_lo, y).
Axes of the slice: x: 4 (x_hi: 2, x_lo: 2; x = x_hi * 2 + x_lo), y: 8, z: 16, core: 2. Of those that a mesh axis runs over, the one named last changes fastest.
Arguments:
- gradient: float32 [64, 256, 512], P(('side', 'grp'), 'shard'), may hold values from -160 to 160
- momentum: float32 [64, 256, 512], P(('side', 'grp'), 'shard'), may hold values from -6 to 6
- master: float32 [64, 256, 512], P(('side', 'grp'), 'shard'), may hold values from -6 to 6
- clip_count: int32 [64], P(('side', 'grp')), may hold values from 0 to 4
- logit_peak: float32 [64], P(('side', 'grp')), may hold values from 150 to 600
- server_map: int32 [64], replicated, may hold values from 0 to 63, each once
Outputs:
- new_master: float32 [64, 256, 512], P(('side', 'grp'), 'shard')
- new_momentum: float32 [64, 256, 512], P(('side', 'grp'), 'shard')
- serving: bfloat16 [64, 256, 512], P('shard')
All inputs are finite; a program needn't handle non-finite values.
Results may differ from a plain program's by a relative error of at most 0.006.
Values may be sent and summed in bfloat16 or wider, within the bound.
No kernel may reach another device: no remote copies, remote signals or barrier semaphores. Data moves between devices by JAX's collectives and lax.ppermute only.
A program may use at most 32 MiB of HBM per device.

v0:
```python
import math

import jax
import jax.numpy as jnp
from jax import lax
from jax.sharding import PartitionSpec as P

KVR = 512
K_NOPE = 128
ITERS = 5


newton_a = 3.4445
newton_b = -4.775
newton_c = 2.0315
momentum_mu = 0.95
learn_rate = 0.5
decay_rate = 0.1
clip_tau = 100.0
epsilon = 1e-07
highest = lax.Precision.HIGHEST


def orthogonal(matrix):
    norm_value = jnp.sqrt(jnp.sum(matrix * matrix, axis=(1, 2))) + epsilon
    current = matrix / norm_value[:, None, None]
    for iteration in range(ITERS):
        gram = jnp.einsum("hrk,hsk->hrs", current, current, precision=highest)
        poly = newton_b * gram + newton_c * jnp.einsum(
            "hrs,hst->hrt", gram, gram, precision=highest
        )
        current = newton_a * current + jnp.einsum("hrs,hsk->hrk", poly, current, precision=highest)
    return current


def shards(gradient, momentum, master, clip_count, logit_peak, server_map):
    new_momentum = momentum_mu * momentum + gradient
    nesterov = gradient + momentum_mu * new_momentum
    row_count = gradient.shape[1]
    shard_pos = lax.axis_index("shard")
    whole_head = lax.all_gather(nesterov.astype(jnp.bfloat16), "shard", axis=1, tiled=True).astype(
        nesterov.dtype
    )
    ortho_whole = orthogonal(whole_head)
    ortho_rows = lax.dynamic_slice_in_dim(ortho_whole, shard_pos * row_count, row_count, 1)
    gamma = jnp.where(clip_count > 0, clip_tau / logit_peak, jnp.ones_like(logit_peak))
    row_index = shard_pos * row_count + jnp.arange(row_count, dtype=jnp.int32)
    factor = jnp.where(
        row_index[None, :, None] < K_NOPE,
        jnp.sqrt(gamma)[:, None, None],
        jnp.ones_like(gamma)[:, None, None],
    )
    updated = (
        (1.0 - learn_rate * decay_rate) * master - learn_rate * 0.2 * math.sqrt(KVR) * ortho_rows
    ) * factor
    head_rows = lax.all_gather(updated.astype(jnp.bfloat16), ("side", "grp"), axis=0, tiled=True)
    ordered = jnp.take(head_rows, server_map, axis=0)
    serving = lax.all_to_all(ordered, "shard", split_axis=0, concat_axis=1, tiled=True)
    return (updated, new_momentum, serving)


def solution(mesh):
    return jax.shard_map(
        shards,
        mesh=mesh,
        in_specs=(
            P(("side", "grp"), "shard", None),
            P(("side", "grp"), "shard", None),
            P(("side", "grp"), "shard", None),
            P(("side", "grp")),
            P(("side", "grp")),
            P(),
        ),
        out_specs=(
            P(("side", "grp"), "shard", None),
            P(("side", "grp"), "shard", None),
            P("shard", None, None),
        ),
        check_vma=False,
    )
```

profile of v0, /device:TPU:1, one launch (start us, length us, event | category | flops | bytes accessed | tf_op | source)
XLA Modules:
  0.0 247.6 jit_solution(12920818404116664579)
XLA Ops:
  7.2 0.0 all-gather.2.cloned.1.call-start
  8.6 1.4 add_convert_fusion
  10.0 28.9 %all_gather.6 = bf16[1,256,512]{2,1,0:T(8,128)(2,1)S(1)} all-gather(bf16[1,16,512]{2,1,0:T(8,128)(2,1)S(1)} %get-tuple-element.5), channel_id=1, replica_groups=mesh['side'=2,'grp'=32,'shard'=16] {'shard'}, dimensions={1}, use_global_device_ids=true | all-gather | bytes 278528 | tf_op jit(solution)/shard_map/all_gather | solution.py:41
  38.9 0.7 fusion.9
  40.3 0.6 fusion.23
  40.9 0.4 fusion.8
  41.3 0.7 fusion
  42.0 0.6 fusion.20
  42.7 0.4 fusion.7
  43.0 0.6 fusion.1
  43.7 0.6 fusion.17
  44.3 0.4 fusion.6
  44.7 0.6 fusion.2
  45.4 0.6 fusion.14
  46.0 0.4 fusion.5
  46.4 0.6 fusion.3
  47.0 0.6 fusion.11
  47.6 0.4 fusion.4
  48.0 0.0 copy-start
  48.1 0.6 convolution_bitcast_fusion
  48.7 0.1 copy-done
  48.8 0.7 fusion.30
  49.5 0.0 copy-start.1
  49.5 0.0 all-gather.2.cloned.1.call-update
  49.5 0.6 copy-done.1
  50.2 156.3 %all-gather.2.cloned.1.call-done = bf16[64,16,512]{2,1,0:T(8,128)(2,1)} async-done(((bf16[1,16,512]{2,1,0:T(8,128)(2,1)}), bf16[64,16,512]{2,1,0:T(8,128)(2,1)}) %all-gather.2.cloned.1.call-update) | async-done | bytes 1048592 | tf_op jit(solution)/shard_map/all_gather | solution.py:56
  206.5 1.8 gather_fusion
  208.3 0.2 broadcast_select_fusion
  208.5 31.2 %all_to_all.18 = bf16[64,16,512]{2,1,0:T(8,128)(2,1)S(1)} all-to-all(bf16[64,16,512]{2,1,0:T(8,128)(2,1)S(1)} %broadcast_select_fusion), channel_id=1, replica_groups=mesh['side'=2,'grp'=32,'shard'=16] {'shard'}, dimensions={0} | all-to-all | bytes 2097152 | tf_op jit(solution)/shard_map/all_to_all | solution.py:58
  239.7 1.1 copy.10
  (4 shorter events, 0.0 us)
Async XLA Ops:
  7.2 199.3 %all-gather.2.cloned.1.call-start = ((), (), s32[]{:S(2)}) async-start(), calls=%async_computation.1 | async-start | bytes 1064960 | tf_op jit(solution)/shard_map/all_gather | solution.py:56
  48.0 0.8 copy-start
  49.5 0.7 copy-start.1
Sparse Core Ops, SparseCore 0:
  49.6 156.7 all-gather.1
where the time goes:
time: 250 us; the launch traced here: 248 us
  waiting for transfers between devices  156 us (62%)
  blocking collectives  60.1 us (24%)
  between operations  16.3 us (7%)
  matrix products  8.25 us (3%)
  local copies, waits for them, and re-layouts  3.65 us (1%)
  other arithmetic  3.01 us (1%)
    all_gather x1, waiting for transfers between devices, shards(): lax.all_gather(updated.astype(jnp.bfloat16), ('side', 'grp'), axis=0, til...  156 us
    all_to_all x1, blocking collectives, shards(): lax.all_to_all(ordered, 'shard', split_axis=0, concat_axis=1, tiled=True)  31.2 us
    all_gather x1, blocking collectives, shards(): lax.all_gather(nesterov.astype(jnp.bfloat16), 'shard', axis=1, tiled=True)  28.9 us
  transfers between devices with their start and end apart: 1, of which 1 were waited for; matrix products, arithmetic and copies ran while one was open for 0% of the time, Pallas kernels for 0%

commit v1 on v0

v1 whole, which is shorter than its diff:
```python
import math

import jax
import jax.numpy as jnp
from jax import lax
from jax.sharding import Mesh
from jax.sharding import PartitionSpec as P

KVR = 512
K_NOPE = 128
ITERS = 5


newton_a = 3.4445
newton_b = -4.775
newton_c = 2.0315
momentum_mu = 0.95
learn_rate = 0.5
decay_rate = 0.1
clip_tau = 100.0
epsilon = 1e-07
highest = lax.Precision.HIGHEST

HEAD_AXES = ("xh", "z", "core")
SHARD_AXIS = "shard"
PARTS = 4


def orthogonal(matrix):
    norm_value = jnp.sqrt(jnp.sum(matrix * matrix)) + epsilon
    current = matrix / norm_value
    for iteration in range(ITERS):
        gram = jnp.dot(current, current.T, precision=highest)
        poly = newton_b * gram + newton_c * jnp.dot(gram, gram, precision=highest)
        current = newton_a * current + jnp.dot(poly, current, precision=highest)
    return current


def shards(gradient, momentum, master, clip_count, logit_peak, server_map):
    new_momentum = momentum_mu * momentum + gradient
    nesterov = gradient + momentum_mu * new_momentum
    _, row_count, columns = gradient.shape
    shard_count = lax.axis_size(SHARD_AXIS)
    z_count = lax.axis_size("z")
    shard_pos = lax.axis_index(SHARD_AXIS)

    own_rows = jnp.broadcast_to(nesterov.astype(jnp.bfloat16), (shard_count, row_count, columns))
    whole_head = lax.all_to_all(own_rows, SHARD_AXIS, 0, 0, tiled=True)
    whole_head = whole_head.reshape(shard_count * row_count, columns).astype(jnp.float32)
    ortho_whole = orthogonal(whole_head)
    ortho_rows = lax.dynamic_slice_in_dim(ortho_whole, shard_pos * row_count, row_count, 0)[None]

    gamma = jnp.where(clip_count > 0, clip_tau / logit_peak, jnp.ones_like(logit_peak))
    row_index = shard_pos * row_count + jnp.arange(row_count, dtype=jnp.int32)
    factor = jnp.where(
        row_index[None, :, None] < K_NOPE,
        jnp.sqrt(gamma)[:, None, None],
        jnp.ones_like(gamma)[:, None, None],
    )
    updated = (
        (1.0 - learn_rate * decay_rate) * master - learn_rate * 0.2 * math.sqrt(KVR) * ortho_rows
    ) * factor

    part_width = columns // PARTS
    parts = updated[0].astype(jnp.bfloat16).reshape(row_count, 2, 2, part_width)
    parts = parts.transpose(2, 1, 0, 3)[:, None]
    sent = jnp.broadcast_to(parts, (2, z_count, 2, row_count, part_width))
    sent = sent.reshape(4 * z_count, row_count, part_width)
    head_parts = lax.all_to_all(sent, HEAD_AXES, 0, 0, tiled=True)
    ordered = jnp.take(head_parts, server_map, axis=0, mode="clip")
    serving = lax.all_to_all(ordered, SHARD_AXIS, split_axis=0, concat_axis=1, tiled=True)
    serving = lax.all_gather(serving, "xh", axis=2, tiled=True)
    serving = lax.all_gather(serving, "core", axis=2, tiled=True)
    return (updated, new_momentum, serving)


def solution(mesh):
    side, grp, shard = (mesh.shape[name] for name in ("side", "grp", "shard"))
    fine = Mesh(
        mesh.devices.reshape(side, grp // 2, 2, shard), ("xh", "z", "core", "shard")
    )
    rows = P(HEAD_AXES, SHARD_AXIS, None)
    return jax.shard_map(
        shards,
        mesh=fine,
        in_specs=(rows, rows, rows, P(HEAD_AXES), P(HEAD_AXES), P()),
        out_specs=(rows, rows, P(SHARD_AXIS, None, None)),
        check_vma=False,
    )
```

time: 250 us -> 133 us (0.53)
  waiting for transfers between devices: 156 us -> 43.7 us
  blocking collectives: 60.1 us -> 23.1 us
  starting transfers between devices: 0.04 us -> 33.7 us
    all_gather x1, waiting for transfers between devices: 156 us -> 13.7 us  [shards(): serving = lax.all_gather(serving, 'core', axis=2, tiled=True)]
    all_to_all x0 -> x2, starting transfers between devices: none -> 33.6 us  [the longest x1 24.9 us: shards(): head_parts = lax.all_to_all(sent, HEAD_AXES, 0, 0, tiled=True)]
    all_to_all x0 -> x2, waiting for transfers between devices: none -> 30 us  [the longest x1 23.7 us: shards(): head_parts = lax.all_to_all(sent, HEAD_AXES, 0, 0, tiled=True)]
    all_gather x1, blocking collectives: 28.9 us -> 9.19 us  [shards(): serving = lax.all_gather(serving, 'xh', axis=2, tiled=True)]
    all_to_all x1, blocking collectives: 31.2 us -> 13.9 us  [shards(): lax.all_to_all(ordered, SHARD_AXIS, split_axis=0, concat_axis=1, tiled=True)]
  transfers between devices with their start and end apart: 1 -> 3, of which waited for: 1 -> 3; matrix products, arithmetic and copies ran while one was open for 0% -> 0% of each run, Pallas kernels for 0% -> 0%
where the time goes in v1:
time: 133 us; the launch traced here: 132 us
  waiting for transfers between devices  43.7 us (33%)
  starting transfers between devices  33.7 us (25%)
  blocking collectives  23.1 us (17%)
  between operations  16.3 us (12%)
  matrix products  8.2 us (6%)
  local copies, waits for them, and re-layouts  4.52 us (3%)
  other arithmetic  2.89 us (2%)
    all_to_all x1, starting transfers between devices, shards(): head_parts = lax.all_to_all(sent, HEAD_AXES, 0, 0, tiled=True)  24.9 us
    all_to_all x1, waiting for transfers between devices, shards(): head_parts = lax.all_to_all(sent, HEAD_AXES, 0, 0, tiled=True)  23.7 us
    all_to_all x1, blocking collectives, shards(): lax.all_to_all(ordered, SHARD_AXIS, split_axis=0, concat_axis=1, tiled=True)  13.9 us
    all_gather x1, waiting for transfers between devices, shards(): serving = lax.all_gather(serving, 'core', axis=2, tiled=True)  13.7 us
    all_gather x1, blocking collectives, shards(): serving = lax.all_gather(serving, 'xh', axis=2, tiled=True)  9.19 us
    all_to_all x1, starting transfers between devices, shards(): whole_head = lax.all_to_all(own_rows, SHARD_AXIS, 0, 0, tiled=True)  8.68 us
    all_to_all x1, waiting for transfers between devices, shards(): whole_head = lax.all_to_all(own_rows, SHARD_AXIS, 0, 0, tiled=True)  6.36 us
    dot_general x5, matrix products, orthogonal(): current = newton_a * current + jnp.dot(poly, current, precision=highest)  3.2 us
  transfers between devices with their start and end apart: 3, of which 3 were waited for; matrix products, arithmetic and copies ran while one was open for 0% of the time, Pallas kernels for 0%

profile of v1, /device:TPU:1, one launch (start us, length us, event | category | flops | bytes accessed | tf_op | source)
XLA Modules:
  0.0 132.4 jit_solution(14823063751475312389)
XLA Ops:
  7.2 1.4 %fusion.10 = (bf16[16,512]{1,0:T(8,128)(2,1)S(1)}, f32[1,16,512]{2,1,0:T(8,128)}) fusion(f32[1,16,512]{2,1,0:T(8,128)} %param.6, f32[1,16,512]{2,1,0:T(8,128)} %param.7), kind=kLoop, calls=%fused_computation.26 | loop fusion | flops 40960 | bytes 114688 | tf_op jit(solution)/shard_map/broadcast_in_dim | solution.py:47
  8.6 0.7 broadcast_in_dim.39
  9.3 8.7 %all-to-all-start = ((bf16[16,16,512]{2,1,0:T(8,128)(2,1)}), bf16[16,16,512]{2,1,0:T(8,128)(2,1)S(1)}, u32[]{:S(2)}, u32[]{:S(2)}) async-start(bf16[16,16,512]{2,1,0:T(8,128)(2,1)} %broadcast_in_dim.39), calls=%async_computation | async-start | bytes 524288 | tf_op jit(solution)/shard_map/all_to_all | solution.py:48
  19.4 6.4 %all-to-all-done = bf16[16,16,512]{2,1,0:T(8,128)(2,1)S(1)} async-done(((bf16[16,16,512]{2,1,0:T(8,128)(2,1)}), bf16[16,16,512]{2,1,0:T(8,128)(2,1)S(1)}, u32[]{:S(2)}, u32[]{:S(2)}) %all-to-all-start) | async-done | bytes 262176 | tf_op jit(solution)/shard_map/all_to_all | solution.py:48
  25.7 0.7 fusion.5
  27.2 0.1 convert_divide_fusion
  27.2 0.6 fusion.13
  27.9 0.4 fusion.4
  28.3 0.6 convolution_add_fusion.3
  28.9 0.6 fusion.14
  29.5 0.4 fusion.3
  29.9 0.6 convolution_add_fusion.2
  30.6 0.6 fusion.15
  31.2 0.4 fusion.2
  31.6 0.6 convolution_add_fusion.1
  32.2 0.6 fusion.16
  32.9 0.4 fusion.1
  33.3 0.6 convolution_add_fusion
  33.9 0.6 fusion.17
  34.5 0.4 fusion
  34.9 0.0 copy-start
  34.9 0.6 fusion.18
  35.6 0.1 copy-done
  35.7 0.7 fusion.11
  36.4 0.7 broadcast_in_dim.43
  37.1 0.0 copy-start.1
  37.1 24.9 %all-to-all-start.1 = ((bf16[64,16,128]{2,1,0:T(8,128)(2,1)}), bf16[64,16,128]{2,1,0:T(8,128)(2,1)S(1)}, u32[]{:S(2)}, u32[]{:S(2)}) async-start(bf16[64,16,128]{2,1,0:T(8,128)(2,1)} %bitcast.5), calls=%async_computation.1 | async-start | bytes 524288 | tf_op jit(solution)/shard_map/all_to_all | solution.py:69
  62.1 0.0 all-gather.2.cloned.1.call-start
  62.1 0.0 copy-done.1
  62.1 23.7 %all-to-all-done.1 = bf16[64,16,128]{2,1,0:T(8,128)(2,1)S(1)} async-done(((bf16[64,16,128]{2,1,0:T(8,128)(2,1)}), bf16[64,16,128]{2,1,0:T(8,128)(2,1)S(1)}, u32[]{:S(2)}, u32[]{:S(2)}) %all-to-all-start.1) | async-done | bytes 262176 | tf_op jit(solution)/shard_map/all_to_all | solution.py:69
  85.8 0.6 gather_fusion
  86.5 13.9 %all_to_all.28 = bf16[64,16,128]{2,1,0:T(8,128)(2,1)S(1)} all-to-all(bf16[64,16,128]{2,1,0:T(8,128)(2,1)S(1)} %gather_fusion), channel_id=1, replica_groups=mesh['xh'=2,'z'=16,'core'=2,'shard'=16] {'shard'}, dimensions={0} | all-to-all | bytes 524288 | tf_op jit(solution)/shard_map/all_to_all | solution.py:71
  100.4 9.2 %all_gather.6 = bf16[4,256,256]{2,1,0:T(8,128)(2,1)} all-gather(bf16[4,256,128]{2,1,0:T(8,128)(2,1)S(1)} %bitcast.49), channel_id=1, replica_groups=mesh['xh'=2,'z'=16,'core'=2,'shard'=16] {'xh'}, dimensions={2}, use_global_device_ids=true | all-gather | bytes 786432 | tf_op jit(solution)/shard_map/all_gather | solution.py:72
  109.6 0.0 all-gather.2.cloned.1.call-update
  109.6 13.7 %all-gather.2.cloned.1.call-done = bf16[4,256,512]{2,1,0:T(8,128)(2,1)} async-done(((bf16[4,256,256]{2,1,0:T(8,128)(2,1)}), bf16[4,256,512]{2,1,0:T(8,128)(2,1)}) %all-gather.2.cloned.1.call-update) | async-done | bytes 1048592 | tf_op jit(solution)/shard_map/all_gather | solution.py:73
  123.2 2.3 %copy.16 = bf16[4,256,512]{2,1,0:T(8,128)(2,1)} copy(bf16[4,256,512]{2,1,0:T(8,128)(2,1)} %all-gather.2.cloned.1.call-done) | data formatting | bytes 2097152
  (5 shorter events, 0.1 us)
Async XLA Ops:
  9.3 16.4 %all-to-all-start = ((bf16[16,16,512]{2,1,0:T(8,128)(2,1)}), bf16[16,16,512]{2,1,0:T(8,128)(2,1)S(1)}, u32[]{:S(2)}, u32[]{:S(2)}) async-start(bf16[16,16,512]{2,1,0:T(8,128)(2,1)} %broadcast_in_dim.39), calls=%async_computation | async-start | bytes 524288 | tf_op jit(solution)/shard_map/all_to_all | solution.py:48
  34.9 0.8 copy-start
  37.1 25.0 %copy-start.1 = (s32[64]{0:T(128)S(1)}, s32[64]{0:T(128)}, u32[]{:S(2)}) copy-start(s32[64]{0:T(128)} %param.11) | copy-start | bytes 772
  37.1 48.7 %all-to-all-start.1 = ((bf16[64,16,128]{2,1,0:T(8,128)(2,1)}), bf16[64,16,128]{2,1,0:T(8,128)(2,1)S(1)}, u32[]{:S(2)}, u32[]{:S(2)}) async-start(bf16[64,16,128]{2,1,0:T(8,128)(2,1)} %bitcast.5), calls=%async_computation.1 | async-start | bytes 524288 | tf_op jit(solution)/shard_map/all_to_all | solution.py:69
  62.1 61.2 %all-gather.2.cloned.1.call-start = ((), (), s32[]{:S(2)}) async-start(), calls=%async_computation.3 | async-start | bytes 1572864 | tf_op jit(solution)/shard_map/all_gather | solution.py:73
Sparse Core Ops, SparseCore 0:
  109.7 13.4 all-gather.1

commit v2 on v1

--- a/solution.py
+++ b/solution.py
@@ -36,6 +36,12 @@
     return current
 
 
+def swap_join(own, axis):
+    other = lax.ppermute(own, axis, [(0, 1), (1, 0)])
+    first = lax.axis_index(axis) == 0
+    return jnp.concatenate([jnp.where(first, own, other), jnp.where(first, other, own)], axis=2)
+
+
 def shards(gradient, momentum, master, clip_count, logit_peak, server_map):
     new_momentum = momentum_mu * momentum + gradient
     nesterov = gradient + momentum_mu * new_momentum
@@ -62,15 +68,16 @@
     ) * factor
 
     part_width = columns // PARTS
-    parts = updated[0].astype(jnp.bfloat16).reshape(row_count, 2, 2, part_width)
-    parts = parts.transpose(2, 1, 0, 3)[:, None]
-    sent = jnp.broadcast_to(parts, (2, z_count, 2, row_count, part_width))
-    sent = sent.reshape(4 * z_count, row_count, part_width)
-    head_parts = lax.all_to_all(sent, HEAD_AXES, 0, 0, tiled=True)
-    ordered = jnp.take(head_parts, server_map, axis=0, mode="clip")
-    serving = lax.all_to_all(ordered, SHARD_AXIS, split_axis=0, concat_axis=1, tiled=True)
-    serving = lax.all_gather(serving, "xh", axis=2, tiled=True)
-    serving = lax.all_gather(serving, "core", axis=2, tiled=True)
+    parts = updated[0].astype(jnp.bfloat16).reshape(row_count, PARTS, part_width).transpose(1, 0, 2)
+    chip_parts = lax.all_to_all(parts, ("core", "xh"), 0, 0, tiled=True)
+    sent = jnp.broadcast_to(chip_parts, (z_count, PARTS, row_count, part_width))
+    head_parts = lax.all_to_all(sent, "z", 0, 0, tiled=True)
+    head_parts = head_parts.reshape(z_count * PARTS, row_count, part_width)
+    half = z_count * 2
+    xh_of, z_of, core_of = server_map // half, (server_map % half) // 2, server_map % 2
+    ordered = jnp.take(head_parts, z_of * PARTS + core_of * 2 + xh_of, axis=0, mode="clip")
+    own = lax.all_to_all(ordered, SHARD_AXIS, split_axis=0, concat_axis=1, tiled=True)
+    serving = swap_join(swap_join(own, "xh"), "core")
     return (updated, new_momentum, serving)
 
 

time: 133 us -> 109 us (0.82)
  waiting for transfers between devices: 43.7 us -> 26.6 us
  between operations: 16.3 us -> 2.96 us
  blocking collectives: 23.1 us -> 28.7 us
  local copies, waits for them, and re-layouts: 4.52 us -> 2.16 us
  starting transfers between devices: 33.7 us -> 35.7 us
  other arithmetic: 2.89 us -> 4.31 us
    all_to_all x0 -> x1, blocking collectives: none -> 17.1 us  [shards(): chip_parts = lax.all_to_all(parts, ('core', 'xh'), 0, 0, tiled=True)]
    ppermute x0 -> x2, starting transfers between devices: none -> 13.8 us  [swap_join(): other = lax.ppermute(own, axis, [(0, 1), (1, 0)])]
    all_gather x1 -> x0, waiting for transfers between devices: 13.7 us -> none  [shards(): serving = lax.all_gather(serving, 'core', axis=2, tiled=True)]
    all_to_all x1, starting transfers between devices: 24.9 us -> 13.2 us  [shards(): head_parts = lax.all_to_all(sent, 'z', 0, 0, tiled=True)]
    all_to_all x1, waiting for transfers between devices: 23.7 us -> 13 us  [shards(): head_parts = lax.all_to_all(sent, 'z', 0, 0, tiled=True)]
    all_gather x1 -> x0, blocking collectives: 9.19 us -> none  [shards(): serving = lax.all_gather(serving, 'xh', axis=2, tiled=True)]
    ppermute x0 -> x2, waiting for transfers between devices: none -> 7.18 us  [swap_join(): other = lax.ppermute(own, axis, [(0, 1), (1, 0)])]
    unnamed x5 -> x4, local copies, waits for them, and re-layouts: 2.39 us -> 0.01 us
  transfers between devices with their start and end apart: 3 -> 4, of which waited for: 3 -> 4; matrix products, arithmetic and copies ran while one was open for 0% -> 0% of each run, Pallas kernels for 0% -> 0%
where the time goes in v2:
time: 109 us
  starting transfers between devices  35.7 us (33%)
  blocking collectives  28.7 us (26%)
  waiting for transfers between devices  26.6 us (24%)
  matrix products  8.19 us (8%)
  other arithmetic  4.31 us (4%)
  between operations  2.96 us (3%)
  local copies, waits for them, and re-layouts  2.16 us (2%)
    all_to_all x1, blocking collectives, shards(): chip_parts = lax.all_to_all(parts, ('core', 'xh'), 0, 0, tiled=True)  17.1 us
    ppermute x2, starting transfers between devices, swap_join(): other = lax.ppermute(own, axis, [(0, 1), (1, 0)])  13.8 us
    all_to_all x1, starting transfers between devices, shards(): head_parts = lax.all_to_all(sent, 'z', 0, 0, tiled=True)  13.2 us
    all_to_all x1, waiting for transfers between devices, shards(): head_parts = lax.all_to_all(sent, 'z', 0, 0, tiled=True)  13 us
    all_to_all x1, blocking collectives, shards(): lax.all_to_all(ordered, SHARD_AXIS, split_axis=0, concat_axis=1, tiled=True)  11.6 us
    all_to_all x1, starting transfers between devices, shards(): whole_head = lax.all_to_all(own_rows, SHARD_AXIS, 0, 0, tiled=True)  8.68 us
    ppermute x2, waiting for transfers between devices, swap_join(): other = lax.ppermute(own, axis, [(0, 1), (1, 0)])  7.18 us
    all_to_all x1, waiting for transfers between devices, shards(): whole_head = lax.all_to_all(own_rows, SHARD_AXIS, 0, 0, tiled=True)  6.36 us
  transfers between devices with their start and end apart: 4, of which 4 were waited for; matrix products, arithmetic and copies ran while one was open for 0% of the time, Pallas kernels for 0%

profile of v2, /device:TPU:1, one launch (start us, length us, event | category | flops | bytes accessed | tf_op | source)
XLA Modules:
  0.0 108.6 jit_solution(7855068493429698825)
XLA Ops:
  0.6 1.4 %fusion.10 = (bf16[16,512]{1,0:T(8,128)(2,1)S(1)}, f32[1,16,512]{2,1,0:T(8,128)}) fusion(f32[1,16,512]{2,1,0:T(8,128)} %param.6, f32[1,16,512]{2,1,0:T(8,128)} %param.7), kind=kLoop, calls=%fused_computation.32 | loop fusion | flops 40960 | bytes 114688 | tf_op jit(solution)/shard_map/broadcast_in_dim | solution.py:53
  2.0 0.7 broadcast_in_dim.36
  2.8 8.7 %all-to-all-start = ((bf16[16,16,512]{2,1,0:T(8,128)(2,1)}), bf16[16,16,512]{2,1,0:T(8,128)(2,1)S(1)}, u32[]{:S(2)}, u32[]{:S(2)}) async-start(bf16[16,16,512]{2,1,0:T(8,128)(2,1)} %broadcast_in_dim.36), calls=%async_computation | async-start | bytes 524288 | tf_op jit(solution)/shard_map/all_to_all | solution.py:54
  12.8 6.4 %all-to-all-done = bf16[16,16,512]{2,1,0:T(8,128)(2,1)S(1)} async-done(((bf16[16,16,512]{2,1,0:T(8,128)(2,1)}), bf16[16,16,512]{2,1,0:T(8,128)(2,1)S(1)}, u32[]{:S(2)}, u32[]{:S(2)}) %all-to-all-start) | async-done | bytes 262176 | tf_op jit(solution)/shard_map/all_to_all | solution.py:54
  19.2 0.7 fusion.5
  20.6 0.1 convert_divide_fusion
  20.7 0.6 fusion.13
  21.3 0.4 fusion.4
  21.7 0.6 convolution_add_fusion.3
  22.4 0.6 fusion.14
  23.0 0.4 fusion.3
  23.4 0.6 convolution_add_fusion.2
  24.0 0.6 fusion.15
  24.7 0.4 fusion.2
  25.1 0.6 convolution_add_fusion.1
  25.7 0.6 fusion.16
  26.3 0.4 fusion.1
  26.7 0.6 convolution_add_fusion
  27.4 0.6 fusion.17
  28.0 0.0 copy-start
  28.0 0.4 fusion
  28.4 0.0 copy-start.1
  28.4 0.6 fusion.18
  29.0 0.0 copy-done
  29.0 0.7 fusion.11
  29.8 17.1 %all_to_all.33 = bf16[4,16,128]{2,1,0:T(8,128)(2,1)S(1)} all-to-all(bf16[4,16,128]{2,1,0:T(8,128)(2,1)S(1)} %bitcast.56), channel_id=1, replica_groups=mesh['xh'=2,'z'=16,'core'=2,'shard'=16] {'core','xh'}, dimensions={0} | all-to-all | bytes 32768 | tf_op jit(solution)/shard_map/all_to_all | solution.py:72
  46.9 0.8 broadcast_in_dim.40
  47.6 13.2 %all-to-all-start.2 = ((bf16[16,4,16,128]{3,2,1,0:T(8,128)(2,1)}), bf16[16,4,16,128]{3,2,1,0:T(8,128)(2,1)S(1)}, u32[]{:S(2)}, u32[]{:S(2)}) async-start(bf16[16,4,16,128]{3,2,1,0:T(8,128)(2,1)} %broadcast_in_dim.40), calls=%async_computation.2 | async-start | bytes 524288 | tf_op jit(solution)/shard_map/all_to_all | solution.py:74
  60.9 0.0 copy-done.1
  60.9 13.0 %all-to-all-done.2 = bf16[16,4,16,128]{3,2,1,0:T(8,128)(2,1)S(1)} async-done(((bf16[16,4,16,128]{3,2,1,0:T(8,128)(2,1)}), bf16[16,4,16,128]{3,2,1,0:T(8,128)(2,1)S(1)}, u32[]{:S(2)}, u32[]{:S(2)}) %all-to-all-start.2) | async-done | bytes 262176 | tf_op jit(solution)/shard_map/all_to_all | solution.py:74
  73.9 0.6 gather_fusion
  74.6 11.6 %all_to_all.34 = bf16[64,16,128]{2,1,0:T(8,128)(2,1)S(1)} all-to-all(bf16[64,16,128]{2,1,0:T(8,128)(2,1)S(1)} %gather_fusion), channel_id=1, replica_groups=mesh['xh'=2,'z'=16,'core'=2,'shard'=16] {'shard'}, dimensions={0} | all-to-all | bytes 524288 | tf_op jit(solution)/shard_map/all_to_all | solution.py:79
  86.2 3.0 %collective-permute-start = (bf16[4,256,128]{2,1,0:T(8,128)(2,1)S(1)}, bf16[4,256,128]{2,1,0:T(8,128)(2,1)S(1)}, u32[]{:S(2)}, u32[]{:S(2)}) collective-permute-start(bf16[4,256,128]{2,1,0:T(8,128)(2,1)S(1)} %bitcast.55), channel_id=1, source_target_pairs={{0,512},{512,0},{1,513},{513,1},{2,514},{514,2},{3,515},{515,3},{4... | collective-permute-start | bytes 786440 | tf_op jit(solution)/shard_map/ppermute | solution.py:40
  89.2 5.7 %collective-permute-done = bf16[4,256,128]{2,1,0:T(8,128)(2,1)S(1)} collective-permute-done((bf16[4,256,128]{2,1,0:T(8,128)(2,1)S(1)}, bf16[4,256,128]{2,1,0:T(8,128)(2,1)S(1)}, u32[]{:S(2)}, u32[]{:S(2)}) %collective-permute-start) | collective-permute-done | bytes 262176 | tf_op jit(solution)/shard_map/ppermute | solution.py:40
  94.9 0.1 broadcast_select_fusion.3
  94.9 0.1 pad_maximum_fusion.1
  95.0 10.8 %collective-permute-start.1 = (bf16[4,256,256]{2,1,0:T(8,128)(2,1)S(1)}, bf16[4,256,256]{2,1,0:T(8,128)(2,1)S(1)}, u32[]{:S(2)}, u32[]{:S(2)}) collective-permute-start(bf16[4,256,256]{2,1,0:T(8,128)(2,1)S(1)} %pad_maximum_fusion.1), channel_id=1, source_target_pairs={{0,16},{16,0},{1,17},{17,1},{2,18},{18,2},{3,19},{19,3},{4,20},{20... | collective-permute-start | bytes 1572872 | tf_op jit(solution)/shard_map/ppermute | solution.py:40
  105.8 1.5 %collective-permute-done.1 = bf16[4,256,256]{2,1,0:T(8,128)(2,1)S(1)} collective-permute-done((bf16[4,256,256]{2,1,0:T(8,128)(2,1)S(1)}, bf16[4,256,256]{2,1,0:T(8,128)(2,1)S(1)}, u32[]{:S(2)}, u32[]{:S(2)}) %collective-permute-start.1) | collective-permute-done | bytes 524320 | tf_op jit(solution)/shard_map/ppermute | solution.py:40
  107.3 0.2 broadcast_select_fusion.1
  107.5 1.1 pad_maximum_fusion
  (6 shorter events, 0.1 us)
Async XLA Ops:
  2.8 16.4 %all-to-all-start = ((bf16[16,16,512]{2,1,0:T(8,128)(2,1)}), bf16[16,16,512]{2,1,0:T(8,128)(2,1)S(1)}, u32[]{:S(2)}, u32[]{:S(2)}) async-start(bf16[16,16,512]{2,1,0:T(8,128)(2,1)} %broadcast_in_dim.36), calls=%async_computation | async-start | bytes 524288 | tf_op jit(solution)/shard_map/all_to_all | solution.py:54
  28.0 1.0 copy-start
  28.4 32.5 %copy-start.1 = (s32[64]{0:T(128)S(1)}, s32[64]{0:T(128)}, u32[]{:S(2)}) copy-start(s32[64]{0:T(128)} %param.11) | copy-start | bytes 772
  47.6 26.3 %all-to-all-start.2 = ((bf16[16,4,16,128]{3,2,1,0:T(8,128)(2,1)}), bf16[16,4,16,128]{3,2,1,0:T(8,128)(2,1)S(1)}, u32[]{:S(2)}, u32[]{:S(2)}) async-start(bf16[16,4,16,128]{3,2,1,0:T(8,128)(2,1)} %broadcast_in_dim.40), calls=%async_computation.2 | async-start | bytes 524288 | tf_op jit(solution)/shard_map/all_to_all | solution.py:74
  86.2 8.7 %collective-permute-start = (bf16[4,256,128]{2,1,0:T(8,128)(2,1)S(1)}, bf16[4,256,128]{2,1,0:T(8,128)(2,1)S(1)}, u32[]{:S(2)}, u32[]{:S(2)}) collective-permute-start(bf16[4,256,128]{2,1,0:T(8,128)(2,1)S(1)} %bitcast.55), channel_id=1, source_target_pairs={{0,512},{512,0},{1,513},{513,1},{2,514},{514,2},{3,515},{515,3},{4... | collective-permute-start | bytes 786440 | tf_op jit(solution)/shard_map/ppermute | solution.py:40
  95.0 12.3 %collective-permute-start.1 = (bf16[4,256,256]{2,1,0:T(8,128)(2,1)S(1)}, bf16[4,256,256]{2,1,0:T(8,128)(2,1)S(1)}, u32[]{:S(2)}, u32[]{:S(2)}) collective-permute-start(bf16[4,256,256]{2,1,0:T(8,128)(2,1)S(1)} %pad_maximum_fusion.1), channel_id=1, source_target_pairs={{0,16},{16,0},{1,17},{17,1},{2,18},{18,2},{3,19},{19,3},{4,20},{20... | collective-permute-start | bytes 1572872 | tf_op jit(solution)/shard_map/ppermute | solution.py:40

commit v3 on v1

v3 whole, which is shorter than its diff:
```python
import math

import jax
import jax.numpy as jnp
from jax import lax
from jax.experimental import pallas as pl
from jax.experimental.pallas import tpu as pltpu
from jax.sharding import Mesh
from jax.sharding import PartitionSpec as P

KVR = 512
K_NOPE = 128
ITERS = 5


newton_a = 3.4445
newton_b = -4.775
newton_c = 2.0315
momentum_mu = 0.95
learn_rate = 0.5
decay_rate = 0.1
clip_tau = 100.0
epsilon = 1e-07

HEAD_AXES = ("xh", "z", "core")
SHARD_AXIS = "shard"
PARTS = 4

VMEM = pl.BlockSpec(memory_space=pltpu.VMEM)
SMEM = pl.BlockSpec(memory_space=pltpu.SMEM)


def dot(left, right):
    return jnp.dot(left, right, preferred_element_type=jnp.float32)


def dot_t(left, right):
    return lax.dot_general(
        left, right, (((1,), (1,)), ((), ())), preferred_element_type=jnp.float32
    )


def split(value):
    high = value.astype(jnp.bfloat16)
    return high, (value - high.astype(jnp.float32)).astype(jnp.bfloat16)


def three(product, left, right):
    return product(left[0], right[0]) + (product(left[0], right[1]) + product(left[1], right[0]))


def refit_kernel(place, count, peak, whole, master, updated, sent, held, gram_held):
    rows = master.shape[1]
    first = pl.multiple_of(place[0] * rows, rows)
    head = whole[...]
    current = head.astype(jnp.float32)
    square = jnp.sum(jnp.sum(current * current, axis=0, keepdims=True), axis=1, keepdims=True)
    scale = 1.0 / (jnp.sqrt(square) + epsilon)
    gram = dot_t(head, head) * scale * scale
    for iteration in range(ITERS - 1):
        pair = split(gram)
        poly = split(newton_b * gram + newton_c * three(dot, pair, pair))
        if iteration == 0:
            current = (newton_a * current + (dot(poly[0], head) + dot(poly[1], head))) * scale
        else:
            current = newton_a * current + three(dot, poly, halves)
        halves = split(current)
        gram = three(dot_t, halves, halves)
    held[...] = current
    gram_held[...] = gram
    gram_rows = gram_held[pl.ds(first, rows), :]
    poly = newton_b * gram_rows + newton_c * three(dot, split(gram_rows), split(gram))
    ortho = newton_a * held[pl.ds(first, rows), :] + three(dot, split(poly), halves)

    shape = ortho.shape
    gamma = jnp.where(count[0] > 0, clip_tau / jnp.full(shape, peak[0], jnp.float32), 1.0)
    row_index = first + lax.broadcasted_iota(jnp.int32, shape, 0)
    factor = jnp.where(row_index < K_NOPE, jnp.sqrt(gamma), 1.0)
    result = (
        (1.0 - learn_rate * decay_rate) * master[0] - learn_rate * 0.2 * math.sqrt(KVR) * ortho
    ) * factor
    updated[0] = result
    narrow = result.astype(jnp.bfloat16)
    places, _, width = sent.shape
    for device in range(places):
        part = device % 2 * 2 + device // (places // 2)
        sent[device] = narrow[:, part * width : (part + 1) * width]


def order_kernel(server_map, parts, ordered):
    slots = parts.shape[0]
    for slot in range(slots):
        part = parts[server_map[slot]]
        ordered[slot] = part
        ordered[slots + slot] = part


def join_kernel(core, own, other, serving, held, sems):
    sides, blocks, slots, rows, width = own.shape

    def fill(slot, lower, upper):
        for half, source in enumerate((lower, upper)):
            for side in range(sides):
                part = half * sides + side
                for block in range(blocks):
                    held[
                        slot, block * rows : (block + 1) * rows, part * width : (part + 1) * width
                    ] = source[side, block, slot]

    for slot in range(slots):

        @pl.when(core[0] == 0)
        def _():
            fill(slot, own, other)

        @pl.when(core[0] != 0)
        def _():
            fill(slot, other, own)

        pltpu.make_async_copy(held.at[slot], serving.at[slot], sems.at[slot]).start()
    for slot in range(slots):
        pltpu.make_async_copy(held.at[slot], serving.at[slot], sems.at[slot]).wait()


def shards(gradient, momentum, master, clip_count, logit_peak, server_map):
    new_momentum = momentum_mu * momentum + gradient
    nesterov = gradient + momentum_mu * new_momentum
    _, row_count, columns = gradient.shape
    shard_count = lax.axis_size(SHARD_AXIS)
    heads = server_map.shape[0]
    slots = heads // shard_count
    width = columns // PARTS
    shard_pos = lax.axis_index(SHARD_AXIS).astype(jnp.int32)[None]
    core_pos = lax.axis_index("core").astype(jnp.int32)[None]

    own_rows = jnp.broadcast_to(nesterov.astype(jnp.bfloat16), (shard_count, row_count, columns))
    whole_head = lax.all_to_all(own_rows, SHARD_AXIS, 0, 0, tiled=True)
    whole_head = whole_head.reshape(shard_count * row_count, columns)

    updated, sent = pl.pallas_call(
        refit_kernel,
        out_shape=(
            jax.ShapeDtypeStruct(master.shape, jnp.float32),
            jax.ShapeDtypeStruct((heads, row_count, width), jnp.bfloat16),
        ),
        in_specs=[SMEM, SMEM, SMEM, VMEM, VMEM],
        out_specs=(VMEM, VMEM),
        scratch_shapes=[
            pltpu.VMEM(whole_head.shape, jnp.float32),
            pltpu.VMEM((whole_head.shape[0],) * 2, jnp.float32),
        ],
    )(shard_pos, clip_count, logit_peak, whole_head, master)

    head_parts = lax.all_to_all(sent, HEAD_AXES, 0, 0, tiled=True)
    ordered = pl.pallas_call(
        order_kernel,
        out_shape=jax.ShapeDtypeStruct((2 * heads, row_count, width), jnp.bfloat16),
        in_specs=[SMEM, VMEM],
        out_specs=VMEM,
    )(server_map, head_parts)
    ordered = ordered.reshape(2 * shard_count, slots, row_count, width)
    own = lax.all_to_all(ordered, ("xh", SHARD_AXIS), 0, 0, tiled=True)
    own = own.reshape(2, shard_count, slots, row_count, width)
    other = lax.ppermute(own, "core", [(0, 1), (1, 0)])
    serving_shape = (slots, shard_count * row_count, columns)
    serving = pl.pallas_call(
        join_kernel,
        out_shape=jax.ShapeDtypeStruct(serving_shape, jnp.bfloat16),
        in_specs=[SMEM, VMEM, VMEM],
        out_specs=pl.BlockSpec(memory_space=pl.ANY),
        scratch_shapes=[
            pltpu.VMEM(serving_shape, jnp.bfloat16),
            pltpu.SemaphoreType.DMA((slots,)),
        ],
    )(core_pos, own, other)
    return (updated, new_momentum, serving)


def solution(mesh):
    side, grp, shard = (mesh.shape[name] for name in ("side", "grp", "shard"))
    fine = Mesh(
        mesh.devices.reshape(side, grp // 2, 2, shard), ("xh", "z", "core", "shard")
    )
    rows = P(HEAD_AXES, SHARD_AXIS, None)
    return jax.shard_map(
        shards,
        mesh=fine,
        in_specs=(rows, rows, rows, P(HEAD_AXES), P(HEAD_AXES), P()),
        out_specs=(rows, rows, P(SHARD_AXIS, None, None)),
        check_vma=False,
    )
```

time: 133 us -> 107 us (0.80)
  blocking collectives: 23.1 us -> 69.5 us
  waiting for transfers between devices: 43.7 us -> 7.97 us
  starting transfers between devices: 33.7 us -> 11.7 us
  between operations: 16.3 us -> 1.95 us
  Pallas kernels: 0 us -> 11.2 us
  matrix products: 8.2 us -> 0 us
  local copies, waits for them, and re-layouts: 4.52 us -> 2.22 us
  other arithmetic: 2.89 us -> 1.4 us
    all_to_all x1 -> x2, blocking collectives: 13.9 us -> 69.5 us  [the longest x1 48.6 us: shards(): head_parts = lax.all_to_all(sent, HEAD_AXES, 0, 0, tiled=True)]
    all_to_all x1 -> x0, starting transfers between devices: 24.9 us -> none  [shards(): head_parts = lax.all_to_all(sent, HEAD_AXES, 0, 0, tiled=True)]
    all_to_all x1 -> x0, waiting for transfers between devices: 23.7 us -> none  [shards(): head_parts = lax.all_to_all(sent, HEAD_AXES, 0, 0, tiled=True)]
    all_gather x1 -> x0, waiting for transfers between devices: 13.7 us -> none  [shards(): serving = lax.all_gather(serving, 'core', axis=2, tiled=True)]
    pallas_call x0 -> x3, Pallas kernels: none -> 11.2 us  [the longest x1 7.1 us: shards(): pl.pallas_call(refit_kernel, out_shape=(jax.ShapeDtypeStruct(master.shape...]
    all_gather x1 -> x0, blocking collectives: 9.19 us -> none  [shards(): serving = lax.all_gather(serving, 'xh', axis=2, tiled=True)]
    dot_general x15 -> x0, matrix products: 8.2 us -> none  [the longest x5 3.2 us: orthogonal(): current = newton_a * current + jnp.dot(poly, current, precision=highest)]
    ppermute x0 -> x1, starting transfers between devices: none -> 3 us  [shards(): other = lax.ppermute(own, 'core', [(0, 1), (1, 0)])]
  transfers between devices with their start and end apart: 3 -> 2, of which waited for: 3 -> 2; matrix products, arithmetic and copies ran while one was open for 0% -> 0% of each run, Pallas kernels for 0% -> 0%
where the time goes in v3:
time: 107 us; the launch traced here: 106 us
  blocking collectives  69.5 us (65%)
  starting transfers between devices  11.7 us (11%)
  Pallas kernels  11.2 us (10%)
  waiting for transfers between devices  7.97 us (7%)
  local copies, waits for them, and re-layouts  2.22 us (2%)
  between operations  1.95 us (2%)
  other arithmetic  1.4 us (1%)
    all_to_all x1, blocking collectives, shards(): head_parts = lax.all_to_all(sent, HEAD_AXES, 0, 0, tiled=True)  48.6 us
    all_to_all x1, blocking collectives, shards(): own = lax.all_to_all(ordered, ('xh', SHARD_AXIS), 0, 0, tiled=True)  20.8 us
    all_to_all x1, starting transfers between devices, shards(): whole_head = lax.all_to_all(own_rows, SHARD_AXIS, 0, 0, tiled=True)  8.68 us
    pallas_call x1, Pallas kernels, shards(): pl.pallas_call(refit_kernel, out_shape=(jax.ShapeDtypeStruct(master.shape...  7.1 us
    all_to_all x1, waiting for transfers between devices, shards(): whole_head = lax.all_to_all(own_rows, SHARD_AXIS, 0, 0, tiled=True)  6.46 us
    ppermute x1, starting transfers between devices, shards(): other = lax.ppermute(own, 'core', [(0, 1), (1, 0)])  3 us
    pallas_call x1, Pallas kernels, shards(): pl.pallas_call(join_kernel, out_shape=jax.ShapeDtypeStruct(serving_shape,...  2.24 us
  transfers between devices with their start and end apart: 2, of which 2 were waited for; matrix products, arithmetic and copies ran while one was open for 0% of the time, Pallas kernels for 0%

profile of v3, /device:TPU:1, one launch (start us, length us, event | category | flops | bytes accessed | tf_op | source)
XLA Modules:
  0.0 105.9 jit_solution(6216446834301538188)
XLA Ops:
  0.6 1.4 %fusion = (bf16[16,512]{1,0:T(8,128)(2,1)S(1)}, f32[1,16,512]{2,1,0:T(8,128)}) fusion(f32[1,16,512]{2,1,0:T(8,128)} %param.6, f32[1,16,512]{2,1,0:T(8,128)} %param.7), kind=kLoop, calls=%fused_computation.2 | loop fusion | flops 40960 | bytes 114688 | tf_op jit(solution)/shard_map/broadcast_in_dim | solution.py:136
  2.0 0.7 broadcast_in_dim.15
  2.8 8.7 %all-to-all-start = ((bf16[16,16,512]{2,1,0:T(8,128)(2,1)}), bf16[16,16,512]{2,1,0:T(8,128)(2,1)S(1)}, u32[]{:S(2)}, u32[]{:S(2)}) async-start(bf16[16,16,512]{2,1,0:T(8,128)(2,1)} %broadcast_in_dim.15), calls=%async_computation | async-start | bytes 524288 | tf_op jit(solution)/shard_map/all_to_all | solution.py:137
  12.7 6.5 %all-to-all-done = bf16[16,16,512]{2,1,0:T(8,128)(2,1)S(1)} async-done(((bf16[16,16,512]{2,1,0:T(8,128)(2,1)}), bf16[16,16,512]{2,1,0:T(8,128)(2,1)S(1)}, u32[]{:S(2)}, u32[]{:S(2)}) %all-to-all-start) | async-done | bytes 262176 | tf_op jit(solution)/shard_map/all_to_all | solution.py:137
  19.2 0.0 copy-start.1
  19.2 0.7 copy-done.1
  19.9 7.1 %shard_map.85 = (f32[1,16,512]{2,1,0:T(8,128)}, bf16[64,16,128]{2,1,0:T(8,128)(2,1)}) custom-call(s32[1]{0:T(128)} %bitcast.place, s32[1]{0:T(128)S(6)} %copy.9.count, f32[1]{0:T(128)S(6)} %copy.10.peak, bf16[256,512]{1,0:T(8,128)(2,1)} %bitcast.10, f32[1,16,512]{2,1,0:T(8,128)} %master.1), custom_call_target="tpu_custom_call" | custom-call | tf_op jit(solution)/shard_map/pallas_call | solution.py:140
  27.0 48.6 %all_to_all.15.parts = bf16[64,16,128]{2,1,0:T(8,128)(2,1)} all-to-all(bf16[64,16,128]{2,1,0:T(8,128)(2,1)} %get-tuple-element.6), channel_id=1, replica_groups=mesh['xh'=2,'z'=16,'core'=2,'shard'=16] {'xh','z','core'}, dimensions={0} | all-to-all | bytes 524288 | tf_op jit(solution)/shard_map/all_to_all | solution.py:154
  75.7 1.9 %shard_map.86 = bf16[128,16,128]{2,1,0:T(8,128)(2,1)} custom-call(s32[64]{0:T(128)} %server_map.1, bf16[64,16,128]{2,1,0:T(8,128)(2,1)} %all_to_all.15.parts), custom_call_target="tpu_custom_call" | custom-call | tf_op jit(solution)/shard_map/pallas_call | solution.py:155
  77.5 20.8 %all_to_all.16 = bf16[32,4,16,128]{3,2,1,0:T(8,128)(2,1)S(1)} all-to-all(bf16[32,4,16,128]{3,2,1,0:T(8,128)(2,1)} %bitcast.9), channel_id=1, replica_groups=mesh['xh'=2,'z'=16,'core'=2,'shard'=16] {'xh','shard'}, dimensions={0} | all-to-all | bytes 1048576 | tf_op jit(solution)/shard_map/all_to_all | solution.py:162
  98.3 0.0 copy-start
  98.3 3.0 %collective-permute-start = (bf16[2,16,4,16,128]{4,3,2,1,0:T(8,128)(2,1)S(1)}, bf16[2,16,4,16,128]{4,3,2,1,0:T(8,128)(2,1)S(1)}, u32[]{:S(2)}, u32[]{:S(2)}) collective-permute-start(bf16[2,16,4,16,128]{4,3,2,1,0:T(8,128)(2,1)S(1)} %bitcast.7), channel_id=1, source_target_pairs={{0,16},{16,0},{1,17},{17,1},{2,18},{18,2},{3,19},{19,3},{4,20},{20... | collective-permute-start | bytes 1572872 | tf_op jit(solution)/shard_map/ppermute | solution.py:164
  101.3 1.5 %collective-permute-done.other = bf16[2,16,4,16,128]{4,3,2,1,0:T(8,128)(2,1)S(1)} collective-permute-done((bf16[2,16,4,16,128]{4,3,2,1,0:T(8,128)(2,1)S(1)}, bf16[2,16,4,16,128]{4,3,2,1,0:T(8,128)(2,1)S(1)}, u32[]{:S(2)}, u32[]{:S(2)}) %collective-permute-start) | collective-permute-done | bytes 524320 | tf_op jit(solution)/shard_map/ppermute | solution.py:164
  102.9 0.0 copy-start.2
  102.9 0.0 copy-done
  102.9 0.8 copy-done.2
  103.6 2.2 %shard_map.87 = bf16[4,256,512]{2,1,0:T(8,128)(2,1)} custom-call(s32[1]{0:T(128)} %bitcast.3.core, bf16[2,16,4,16,128]{4,3,2,1,0:T(8,128)(2,1)} %bitcast.8, bf16[2,16,4,16,128]{4,3,2,1,0:T(8,128)(2,1)} %copy-done.2), custom_call_target="tpu_custom_call" | custom-call | tf_op jit(solution)/shard_map/pallas_call | solution.py:166
Async XLA Ops:
  2.8 16.4 %all-to-all-start = ((bf16[16,16,512]{2,1,0:T(8,128)(2,1)}), bf16[16,16,512]{2,1,0:T(8,128)(2,1)S(1)}, u32[]{:S(2)}, u32[]{:S(2)}) async-start(bf16[16,16,512]{2,1,0:T(8,128)(2,1)} %broadcast_in_dim.15), calls=%async_computation | async-start | bytes 524288 | tf_op jit(solution)/shard_map/all_to_all | solution.py:137
  19.2 0.7 copy-start.1
  98.3 4.5 %copy-start = (bf16[32,4,16,128]{3,2,1,0:T(8,128)(2,1)}, bf16[32,4,16,128]{3,2,1,0:T(8,128)(2,1)S(1)}, u32[]{:S(2)}) copy-start(bf16[32,4,16,128]{3,2,1,0:T(8,128)(2,1)S(1)} %all_to_all.16) | copy-start | bytes 1572868
  98.3 4.5 %collective-permute-start = (bf16[2,16,4,16,128]{4,3,2,1,0:T(8,128)(2,1)S(1)}, bf16[2,16,4,16,128]{4,3,2,1,0:T(8,128)(2,1)S(1)}, u32[]{:S(2)}, u32[]{:S(2)}) collective-permute-start(bf16[2,16,4,16,128]{4,3,2,1,0:T(8,128)(2,1)S(1)} %bitcast.7), channel_id=1, source_target_pairs={{0,16},{16,0},{1,17},{17,1},{2,18},{18,2},{3,19},{19,3},{4,20},{20... | collective-permute-start | bytes 1572872 | tf_op jit(solution)/shard_map/ppermute | solution.py:164
  102.9 0.8 copy-start.2

commit v4 on v3

--- a/solution.py
+++ b/solution.py
@@ -28,6 +28,8 @@
 
 VMEM = pl.BlockSpec(memory_space=pltpu.VMEM)
 SMEM = pl.BlockSpec(memory_space=pltpu.SMEM)
+LARGE = pltpu.CompilerParams(vmem_limit_bytes=12 << 20)
+SMALL = pltpu.CompilerParams(vmem_limit_bytes=6 << 20)
 
 
 def dot(left, right):
@@ -47,6 +49,11 @@
 
 def three(product, left, right):
     return product(left[0], right[0]) + (product(left[0], right[1]) + product(left[1], right[0]))
+
+
+def three_gram(pair, product):
+    cross = product(pair[0], pair[1])
+    return product(pair[0], pair[0]) + (cross + cross.T)
 
 
 def refit_kernel(place, count, peak, whole, master, updated, sent, held, gram_held):
@@ -59,13 +66,13 @@
     gram = dot_t(head, head) * scale * scale
     for iteration in range(ITERS - 1):
         pair = split(gram)
-        poly = split(newton_b * gram + newton_c * three(dot, pair, pair))
+        poly = split(newton_b * gram + newton_c * three_gram(pair, dot))
         if iteration == 0:
             current = (newton_a * current + (dot(poly[0], head) + dot(poly[1], head))) * scale
         else:
             current = newton_a * current + three(dot, poly, halves)
         halves = split(current)
-        gram = three(dot_t, halves, halves)
+        gram = three_gram(halves, dot_t)
     held[...] = current
     gram_held[...] = gram
     gram_rows = gram_held[pl.ds(first, rows), :]
@@ -149,6 +156,7 @@
             pltpu.VMEM(whole_head.shape, jnp.float32),
             pltpu.VMEM((whole_head.shape[0],) * 2, jnp.float32),
         ],
+        compiler_params=LARGE,
     )(shard_pos, clip_count, logit_peak, whole_head, master)
 
     head_parts = lax.all_to_all(sent, HEAD_AXES, 0, 0, tiled=True)
@@ -157,6 +165,7 @@
         out_shape=jax.ShapeDtypeStruct((2 * heads, row_count, width), jnp.bfloat16),
         in_specs=[SMEM, VMEM],
         out_specs=VMEM,
+        compiler_params=SMALL,
     )(server_map, head_parts)
     ordered = ordered.reshape(2 * shard_count, slots, row_count, width)
     own = lax.all_to_all(ordered, ("xh", SHARD_AXIS), 0, 0, tiled=True)
@@ -172,6 +181,7 @@
             pltpu.VMEM(serving_shape, jnp.bfloat16),
             pltpu.SemaphoreType.DMA((slots,)),
         ],
+        compiler_params=SMALL,
     )(core_pos, own, other)
     return (updated, new_momentum, serving)
 

time: 107 us -> 101 us (0.944)
  Pallas kernels: 11.2 us -> 7.01 us
  local copies, waits for them, and re-layouts: 2.22 us -> 0.74 us
    pallas_call x1, Pallas kernels: 7.1 us -> 5.34 us  [shards(): pl.pallas_call(refit_kernel, out_shape=(jax.ShapeDtypeStruct(master.shape...]
    unnamed x6 -> x4, local copies, waits for them, and re-layouts: 1.49 us -> 0.01 us
    pallas_call x1, Pallas kernels: 1.85 us -> 0.63 us  [shards(): pl.pallas_call(order_kernel, out_shape=jax.ShapeDtypeStruct((2 * heads, r...]
    pallas_call x1, Pallas kernels: 2.24 us -> 1.04 us  [shards(): pl.pallas_call(join_kernel, out_shape=jax.ShapeDtypeStruct(serving_shape,...]
where the time goes in v4:
time: 101 us; the launch traced here: 100 us
  blocking collectives  69.1 us (68%)
  starting transfers between devices  11.8 us (12%)
  waiting for transfers between devices  7.97 us (8%)
  Pallas kernels  7.01 us (7%)
  between operations  1.96 us (2%)
  other arithmetic  1.4 us (1%)
    all_to_all x1, blocking collectives, shards(): head_parts = lax.all_to_all(sent, HEAD_AXES, 0, 0, tiled=True)  48.5 us
    all_to_all x1, blocking collectives, shards(): own = lax.all_to_all(ordered, ('xh', SHARD_AXIS), 0, 0, tiled=True)  20.6 us
    all_to_all x1, starting transfers between devices, shards(): whole_head = lax.all_to_all(own_rows, SHARD_AXIS, 0, 0, tiled=True)  8.81 us
    all_to_all x1, waiting for transfers between devices, shards(): whole_head = lax.all_to_all(own_rows, SHARD_AXIS, 0, 0, tiled=True)  6.46 us
    pallas_call x1, Pallas kernels, shards(): pl.pallas_call(refit_kernel, out_shape=(jax.ShapeDtypeStruct(master.shape...  5.34 us
    ppermute x1, starting transfers between devices, shards(): other = lax.ppermute(own, 'core', [(0, 1), (1, 0)])  3 us
  transfers between devices with their start and end apart: 2, of which 2 were waited for; matrix products, arithmetic and copies ran while one was open for 0% of the time, Pallas kernels for 0%

profile of v4, /device:TPU:1, one launch (start us, length us, event | category | flops | bytes accessed | tf_op | source)
XLA Modules:
  0.0 100.0 jit_solution(12519079218568385428)
XLA Ops:
  0.6 1.4 %fusion = (bf16[16,512]{1,0:T(8,128)(2,1)S(1)}, f32[1,16,512]{2,1,0:T(8,128)}) fusion(f32[1,16,512]{2,1,0:T(8,128)} %param.6, f32[1,16,512]{2,1,0:T(8,128)} %param.7), kind=kLoop, calls=%fused_computation.2 | loop fusion | flops 40960 | bytes 114688 | tf_op jit(solution)/shard_map/broadcast_in_dim | solution.py:143
  2.0 0.7 broadcast_in_dim.15
  2.8 0.0 copy-start
  2.8 8.8 %all-to-all-start = ((bf16[16,16,512]{2,1,0:T(8,128)(2,1)}), bf16[16,16,512]{2,1,0:T(8,128)(2,1)S(1)}, u32[]{:S(2)}, u32[]{:S(2)}) async-start(bf16[16,16,512]{2,1,0:T(8,128)(2,1)} %broadcast_in_dim.15), calls=%async_computation | async-start | bytes 524288 | tf_op jit(solution)/shard_map/all_to_all | solution.py:144
  12.9 6.5 %all-to-all-done = bf16[16,16,512]{2,1,0:T(8,128)(2,1)S(1)} async-done(((bf16[16,16,512]{2,1,0:T(8,128)(2,1)}), bf16[16,16,512]{2,1,0:T(8,128)(2,1)S(1)}, u32[]{:S(2)}, u32[]{:S(2)}) %all-to-all-start) | async-done | bytes 262176 | tf_op jit(solution)/shard_map/all_to_all | solution.py:144
  19.3 0.0 copy-done
  19.3 5.3 %shard_map.85 = (f32[1,16,512]{2,1,0:T(8,128)}, bf16[64,16,128]{2,1,0:T(8,128)(2,1)S(1)}) custom-call(s32[1]{0:T(128)} %bitcast.place, s32[1]{0:T(128)S(6)} %copy.9.count, f32[1]{0:T(128)S(6)} %copy.10.peak, bf16[256,512]{1,0:T(8,128)(2,1)S(1)} %bitcast.10, f32[1,16,512]{2,1,0:T(8,128)S(1)} %copy-done), custom_call_target="tpu_custom_call" | custom-call | tf_op jit(solution)/shard_map/pallas_call | solution.py:147
  24.7 0.0 copy-start.1
  24.7 48.5 %all_to_all.15.parts = bf16[64,16,128]{2,1,0:T(8,128)(2,1)S(1)} all-to-all(bf16[64,16,128]{2,1,0:T(8,128)(2,1)S(1)} %get-tuple-element.6), channel_id=1, replica_groups=mesh['xh'=2,'z'=16,'core'=2,'shard'=16] {'xh','z','core'}, dimensions={0} | all-to-all | bytes 524288 | tf_op jit(solution)/shard_map/all_to_all | solution.py:162
  73.2 0.0 copy-done.1
  73.2 0.6 shard_map.86
  73.8 20.6 %all_to_all.16 = bf16[32,4,16,128]{3,2,1,0:T(8,128)(2,1)S(1)} all-to-all(bf16[32,4,16,128]{3,2,1,0:T(8,128)(2,1)S(1)} %bitcast.9), channel_id=1, replica_groups=mesh['xh'=2,'z'=16,'core'=2,'shard'=16] {'xh','shard'}, dimensions={0} | all-to-all | bytes 1048576 | tf_op jit(solution)/shard_map/all_to_all | solution.py:171
  94.4 3.0 %collective-permute-start = (bf16[2,16,4,16,128]{4,3,2,1,0:T(8,128)(2,1)S(1)}, bf16[2,16,4,16,128]{4,3,2,1,0:T(8,128)(2,1)S(1)}, u32[]{:S(2)}, u32[]{:S(2)}) collective-permute-start(bf16[2,16,4,16,128]{4,3,2,1,0:T(8,128)(2,1)S(1)} %bitcast.7), channel_id=1, source_target_pairs={{0,16},{16,0},{1,17},{17,1},{2,18},{18,2},{3,19},{19,3},{4,20},{20... | collective-permute-start | bytes 1572872 | tf_op jit(solution)/shard_map/ppermute | solution.py:173
  97.5 1.5 %collective-permute-done.other = bf16[2,16,4,16,128]{4,3,2,1,0:T(8,128)(2,1)S(1)} collective-permute-done((bf16[2,16,4,16,128]{4,3,2,1,0:T(8,128)(2,1)S(1)}, bf16[2,16,4,16,128]{4,3,2,1,0:T(8,128)(2,1)S(1)}, u32[]{:S(2)}, u32[]{:S(2)}) %collective-permute-start) | collective-permute-done | bytes 524320 | tf_op jit(solution)/shard_map/ppermute | solution.py:173
  99.0 1.0 %shard_map.87 = bf16[4,256,512]{2,1,0:T(8,128)(2,1)} custom-call(s32[1]{0:T(128)} %bitcast.3.core, bf16[2,16,4,16,128]{4,3,2,1,0:T(8,128)(2,1)S(1)} %bitcast.8, bf16[2,16,4,16,128]{4,3,2,1,0:T(8,128)(2,1)S(1)} %collective-permute-done.other), custom_call_target="tpu_custom_call" | custom-call | tf_op jit(solution)/shard_map/pallas_call | solution.py:175
Async XLA Ops:
  2.8 16.6 %copy-start = (f32[1,16,512]{2,1,0:T(8,128)S(1)}, f32[1,16,512]{2,1,0:T(8,128)}, u32[]{:S(2)}) copy-start(f32[1,16,512]{2,1,0:T(8,128)} %master.1) | copy-start | bytes 98308
  2.8 16.6 %all-to-all-start = ((bf16[16,16,512]{2,1,0:T(8,128)(2,1)}), bf16[16,16,512]{2,1,0:T(8,128)(2,1)S(1)}, u32[]{:S(2)}, u32[]{:S(2)}) async-start(bf16[16,16,512]{2,1,0:T(8,128)(2,1)} %broadcast_in_dim.15), calls=%async_computation | async-start | bytes 524288 | tf_op jit(solution)/shard_map/all_to_all | solution.py:144
  24.7 48.5 %copy-start.1 = (s32[64]{0:T(128)S(1)}, s32[64]{0:T(128)}, u32[]{:S(2)}) copy-start(s32[64]{0:T(128)} %server_map.1) | copy-start | bytes 772
  94.4 4.5 %collective-permute-start = (bf16[2,16,4,16,128]{4,3,2,1,0:T(8,128)(2,1)S(1)}, bf16[2,16,4,16,128]{4,3,2,1,0:T(8,128)(2,1)S(1)}, u32[]{:S(2)}, u32[]{:S(2)}) collective-permute-start(bf16[2,16,4,16,128]{4,3,2,1,0:T(8,128)(2,1)S(1)} %bitcast.7), channel_id=1, source_target_pairs={{0,16},{16,0},{1,17},{17,1},{2,18},{18,2},{3,19},{19,3},{4,20},{20... | collective-permute-start | bytes 1572872 | tf_op jit(solution)/shard_map/ppermute | solution.py:173

commit v5 on v4

--- a/solution.py
+++ b/solution.py
@@ -22,8 +22,9 @@
 clip_tau = 100.0
 epsilon = 1e-07
 
-HEAD_AXES = ("xh", "z", "core")
+HEAD_AXES = ("xh", "zh", "zl", "core")
 SHARD_AXIS = "shard"
+SHARERS = ("xh", "zl")
 PARTS = 4
 
 VMEM = pl.BlockSpec(memory_space=pltpu.VMEM)
@@ -87,23 +88,23 @@
         (1.0 - learn_rate * decay_rate) * master[0] - learn_rate * 0.2 * math.sqrt(KVR) * ortho
     ) * factor
     updated[0] = result
-    narrow = result.astype(jnp.bfloat16)
-    places, _, width = sent.shape
+    places, height, width = sent.shape
+    narrow = [
+        result[half * height : (half + 1) * height].astype(jnp.bfloat16) for half in range(2)
+    ]
     for device in range(places):
         part = device % 2 * 2 + device // (places // 2)
-        sent[device] = narrow[:, part * width : (part + 1) * width]
+        sent[device] = narrow[device // 2 % 2][:, part * width : (part + 1) * width]
 
 
 def order_kernel(server_map, parts, ordered):
-    slots = parts.shape[0]
-    for slot in range(slots):
-        part = parts[server_map[slot]]
-        ordered[slot] = part
-        ordered[slots + slot] = part
+    for slot in range(parts.shape[0]):
+        ordered[slot] = parts[server_map[slot]]
 
 
 def join_kernel(core, own, other, serving, held, sems):
-    sides, blocks, slots, rows, width = own.shape
+    sides, _, blocks, slots, height, width = own.shape
+    rows = 2 * height
 
     def fill(slot, lower, upper):
         for half, source in enumerate((lower, upper)):
@@ -112,7 +113,9 @@
                 for block in range(blocks):
                     held[
                         slot, block * rows : (block + 1) * rows, part * width : (part + 1) * width
-                    ] = source[side, block, slot]
+                    ] = jnp.concatenate(
+                        [source[side, 0, block, slot], source[side, 1, block, slot]], axis=0
+                    )
 
     for slot in range(slots):
 
@@ -136,7 +139,7 @@
     shard_count = lax.axis_size(SHARD_AXIS)
     heads = server_map.shape[0]
     slots = heads // shard_count
-    width = columns // PARTS
+    width, height = columns // PARTS, row_count // 2
     shard_pos = lax.axis_index(SHARD_AXIS).astype(jnp.int32)[None]
     core_pos = lax.axis_index("core").astype(jnp.int32)[None]
 
@@ -148,7 +151,7 @@
         refit_kernel,
         out_shape=(
             jax.ShapeDtypeStruct(master.shape, jnp.float32),
-            jax.ShapeDtypeStruct((heads, row_count, width), jnp.bfloat16),
+            jax.ShapeDtypeStruct((heads, height, width), jnp.bfloat16),
         ),
         in_specs=[SMEM, SMEM, SMEM, VMEM, VMEM],
         out_specs=(VMEM, VMEM),
@@ -162,14 +165,16 @@
     head_parts = lax.all_to_all(sent, HEAD_AXES, 0, 0, tiled=True)
     ordered = pl.pallas_call(
         order_kernel,
-        out_shape=jax.ShapeDtypeStruct((2 * heads, row_count, width), jnp.bfloat16),
+        out_shape=jax.ShapeDtypeStruct(head_parts.shape, jnp.bfloat16),
         in_specs=[SMEM, VMEM],
         out_specs=VMEM,
         compiler_params=SMALL,
     )(server_map, head_parts)
-    ordered = ordered.reshape(2 * shard_count, slots, row_count, width)
-    own = lax.all_to_all(ordered, ("xh", SHARD_AXIS), 0, 0, tiled=True)
-    own = own.reshape(2, shard_count, slots, row_count, width)
+    ordered = ordered.reshape(shard_count, slots, height, width)
+    own = lax.all_to_all(ordered, SHARD_AXIS, 0, 0, tiled=True)
+    own = jnp.broadcast_to(own, (PARTS, *own.shape))
+    own = lax.all_to_all(own, SHARERS, 0, 0, tiled=True)
+    own = own.reshape(2, 2, shard_count, slots, height, width)
     other = lax.ppermute(own, "core", [(0, 1), (1, 0)])
     serving_shape = (slots, shard_count * row_count, columns)
     serving = pl.pallas_call(
@@ -189,7 +194,7 @@
 def solution(mesh):
     side, grp, shard = (mesh.shape[name] for name in ("side", "grp", "shard"))
     fine = Mesh(
-        mesh.devices.reshape(side, grp // 2, 2, shard), ("xh", "z", "core", "shard")
+        mesh.devices.reshape(side, grp // 4, 2, 2, shard), (*HEAD_AXES, SHARD_AXIS)
     )
     rows = P(HEAD_AXES, SHARD_AXIS, None)
     return jax.shard_map(

time: 101 us -> 98.4 us (0.974)
  blocking collectives: 69.1 us -> 64.5 us
  starting transfers between devices: 11.8 us -> 14.2 us
    all_to_all x1, blocking collectives: 48.5 us -> 43.4 us  [shards(): head_parts = lax.all_to_all(sent, HEAD_AXES, 0, 0, tiled=True)]
    ppermute x1, starting transfers between devices: 3 us -> 5.4 us  [shards(): other = lax.ppermute(own, 'core', [(0, 1), (1, 0)])]
    all_to_all x1 -> x2, blocking collectives: 20.6 us -> 21.2 us  [the longest x1 11.3 us: shards(): own = lax.all_to_all(ordered, SHARD_AXIS, 0, 0, tiled=True)]
where the time goes in v5:
time: 98.4 us; the launch traced here: 97.9 us
  blocking collectives  64.5 us (66%)
  starting transfers between devices  14.2 us (14%)
  waiting for transfers between devices  7.97 us (8%)
  Pallas kernels  6.98 us (7%)
  between operations  1.97 us (2%)
  other arithmetic  1.4 us (1%)
    all_to_all x1, blocking collectives, shards(): head_parts = lax.all_to_all(sent, HEAD_AXES, 0, 0, tiled=True)  43.4 us
    all_to_all x1, blocking collectives, shards(): own = lax.all_to_all(ordered, SHARD_AXIS, 0, 0, tiled=True)  11.3 us
    all_to_all x1, blocking collectives, shards(): own = lax.all_to_all(own, SHARERS, 0, 0, tiled=True)  9.88 us
    all_to_all x1, starting transfers between devices, shards(): whole_head = lax.all_to_all(own_rows, SHARD_AXIS, 0, 0, tiled=True)  8.81 us
    all_to_all x1, waiting for transfers between devices, shards(): whole_head = lax.all_to_all(own_rows, SHARD_AXIS, 0, 0, tiled=True)  6.46 us
    ppermute x1, starting transfers between devices, shards(): other = lax.ppermute(own, 'core', [(0, 1), (1, 0)])  5.4 us
    pallas_call x1, Pallas kernels, shards(): pl.pallas_call(refit_kernel, out_shape=(jax.ShapeDtypeStruct(master.shape...  5.35 us
  transfers between devices with their start and end apart: 2, of which 2 were waited for; matrix products, arithmetic and copies ran while one was open for 0% of the time, Pallas kernels for 0%

profile of v5, /device:TPU:1, one launch (start us, length us, event | category | flops | bytes accessed | tf_op | source)
XLA Modules:
  0.0 97.9 jit_solution(11981479051088122402)
XLA Ops:
  0.6 1.4 %fusion = (bf16[16,512]{1,0:T(8,128)(2,1)S(1)}, f32[1,16,512]{2,1,0:T(8,128)}) fusion(f32[1,16,512]{2,1,0:T(8,128)} %param.6, f32[1,16,512]{2,1,0:T(8,128)} %param.7), kind=kLoop, calls=%fused_computation.2 | loop fusion | flops 40960 | bytes 114688 | tf_op jit(solution)/shard_map/broadcast_in_dim | solution.py:146
  2.0 0.7 broadcast_in_dim.18
  2.8 0.0 copy-start
  2.8 8.8 %all-to-all-start = ((bf16[16,16,512]{2,1,0:T(8,128)(2,1)}), bf16[16,16,512]{2,1,0:T(8,128)(2,1)S(1)}, u32[]{:S(2)}, u32[]{:S(2)}) async-start(bf16[16,16,512]{2,1,0:T(8,128)(2,1)} %broadcast_in_dim.18), calls=%async_computation | async-start | bytes 524288 | tf_op jit(solution)/shard_map/all_to_all | solution.py:147
  12.9 6.5 %all-to-all-done = bf16[16,16,512]{2,1,0:T(8,128)(2,1)S(1)} async-done(((bf16[16,16,512]{2,1,0:T(8,128)(2,1)}), bf16[16,16,512]{2,1,0:T(8,128)(2,1)S(1)}, u32[]{:S(2)}, u32[]{:S(2)}) %all-to-all-start) | async-done | bytes 262176 | tf_op jit(solution)/shard_map/all_to_all | solution.py:147
  19.3 0.0 copy-done
  19.3 5.3 %shard_map.85 = (f32[1,16,512]{2,1,0:T(8,128)}, bf16[64,8,128]{2,1,0:T(8,128)(2,1)S(1)}) custom-call(s32[1]{0:T(128)} %bitcast.place, s32[1]{0:T(128)S(6)} %copy.9.count, f32[1]{0:T(128)S(6)} %copy.10.peak, bf16[256,512]{1,0:T(8,128)(2,1)S(1)} %bitcast.9, f32[1,16,512]{2,1,0:T(8,128)S(1)} %copy-done), custom_call_target="tpu_custom_call" | custom-call | tf_op jit(solution)/shard_map/pallas_call | solution.py:150
  24.7 0.0 copy-start.1
  24.7 43.4 %all_to_all.20.parts = bf16[64,8,128]{2,1,0:T(8,128)(2,1)S(1)} all-to-all(bf16[64,8,128]{2,1,0:T(8,128)(2,1)S(1)} %get-tuple-element.6), channel_id=1, replica_groups=mesh['xh'=2,'zh'=8,'zl'=2,'core'=2,'shard'=16] {'xh','zh','zl','core'}, dimensions={0} | all-to-all | bytes 262144 | tf_op jit(solution)/shard_map/all_to_all | solution.py:165
  68.1 0.0 copy-done.1
  68.1 0.6 shard_map.86
  68.7 11.3 %all_to_all.21 = bf16[16,4,8,128]{3,2,1,0:T(8,128)(2,1)S(1)} all-to-all(bf16[16,4,8,128]{3,2,1,0:T(8,128)(2,1)S(1)} %bitcast.10), channel_id=1, replica_groups=mesh['xh'=2,'zh'=8,'zl'=2,'core'=2,'shard'=16] {'shard'}, dimensions={0} | all-to-all | bytes 262144 | tf_op jit(solution)/shard_map/all_to_all | solution.py:174
  79.9 0.1 broadcast_in_dim.20
  80.0 9.9 %all_to_all.22 = bf16[4,16,4,8,128]{4,3,2,1,0:T(8,128)(2,1)S(1)} all-to-all(bf16[4,16,4,8,128]{4,3,2,1,0:T(8,128)(2,1)S(1)} %broadcast_in_dim.20), channel_id=1, replica_groups=mesh['xh'=2,'zh'=8,'zl'=2,'core'=2,'shard'=16] {'xh','zl'}, dimensions={0} | all-to-all | bytes 1048576 | tf_op jit(solution)/shard_map/all_to_all | solution.py:176
  89.9 5.4 %collective-permute-start = (bf16[2,2,16,4,8,128]{5,4,3,2,1,0:T(8,128)(2,1)S(1)}, bf16[2,2,16,4,8,128]{5,4,3,2,1,0:T(8,128)(2,1)S(1)}, u32[]{:S(2)}, u32[]{:S(2)}) collective-permute-start(bf16[2,2,16,4,8,128]{5,4,3,2,1,0:T(8,128)(2,1)S(1)} %bitcast.7), channel_id=1, source_target_pairs={{0,16},{16,0},{1,17},{17,1},{2,18},{18,2},{3,19},{19,3},{4,20},{20... | collective-permute-start | bytes 1572872 | tf_op jit(solution)/shard_map/ppermute | solution.py:178
  95.3 1.5 %collective-permute-done.other = bf16[2,2,16,4,8,128]{5,4,3,2,1,0:T(8,128)(2,1)S(1)} collective-permute-done((bf16[2,2,16,4,8,128]{5,4,3,2,1,0:T(8,128)(2,1)S(1)}, bf16[2,2,16,4,8,128]{5,4,3,2,1,0:T(8,128)(2,1)S(1)}, u32[]{:S(2)}, u32[]{:S(2)}) %collective-permute-start) | collective-permute-done | bytes 524320 | tf_op jit(solution)/shard_map/ppermute | solution.py:178
  96.8 1.0 %shard_map.87 = bf16[4,256,512]{2,1,0:T(8,128)(2,1)} custom-call(s32[1]{0:T(128)} %bitcast.3.core, bf16[2,2,16,4,8,128]{5,4,3,2,1,0:T(8,128)(2,1)S(1)} %bitcast.8, bf16[2,2,16,4,8,128]{5,4,3,2,1,0:T(8,128)(2,1)S(1)} %collective-permute-done.other), custom_call_target="tpu_custom_call" | custom-call | tf_op jit(solution)/shard_map/pallas_call | solution.py:180
Async XLA Ops:
  2.8 16.6 %copy-start = (f32[1,16,512]{2,1,0:T(8,128)S(1)}, f32[1,16,512]{2,1,0:T(8,128)}, u32[]{:S(2)}) copy-start(f32[1,16,512]{2,1,0:T(8,128)} %master.1) | copy-start | bytes 98308
  2.8 16.6 %all-to-all-start = ((bf16[16,16,512]{2,1,0:T(8,128)(2,1)}), bf16[16,16,512]{2,1,0:T(8,128)(2,1)S(1)}, u32[]{:S(2)}, u32[]{:S(2)}) async-start(bf16[16,16,512]{2,1,0:T(8,128)(2,1)} %broadcast_in_dim.18), calls=%async_computation | async-start | bytes 524288 | tf_op jit(solution)/shard_map/all_to_all | solution.py:147
  24.7 43.4 %copy-start.1 = (s32[64]{0:T(128)S(1)}, s32[64]{0:T(128)}, u32[]{:S(2)}) copy-start(s32[64]{0:T(128)} %server_map.1) | copy-start | bytes 772
  89.9 6.9 %collective-permute-start = (bf16[2,2,16,4,8,128]{5,4,3,2,1,0:T(8,128)(2,1)S(1)}, bf16[2,2,16,4,8,128]{5,4,3,2,1,0:T(8,128)(2,1)S(1)}, u32[]{:S(2)}, u32[]{:S(2)}) collective-permute-start(bf16[2,2,16,4,8,128]{5,4,3,2,1,0:T(8,128)(2,1)S(1)} %bitcast.7), channel_id=1, source_target_pairs={{0,16},{16,0},{1,17},{17,1},{2,18},{18,2},{3,19},{19,3},{4,20},{20... | collective-permute-start | bytes 1572872 | tf_op jit(solution)/shard_map/ppermute | solution.py:178

commit v6 on v5

--- a/solution.py
+++ b/solution.py
@@ -28,7 +28,9 @@
 PARTS = 4
 
 VMEM = pl.BlockSpec(memory_space=pltpu.VMEM)
+HBM = pl.BlockSpec(memory_space=pltpu.HBM)
 SMEM = pl.BlockSpec(memory_space=pltpu.SMEM)
+WHOLE = pltpu.CompilerParams(vmem_limit_bytes=60 << 20)
 LARGE = pltpu.CompilerParams(vmem_limit_bytes=12 << 20)
 SMALL = pltpu.CompilerParams(vmem_limit_bytes=6 << 20)
 
@@ -52,33 +54,71 @@
     return product(left[0], right[0]) + (product(left[0], right[1]) + product(left[1], right[0]))
 
 
-def three_gram(pair, product):
-    cross = product(pair[0], pair[1])
-    return product(pair[0], pair[0]) + (cross + cross.T)
+def symmetric(pairs, product):
+    main = sum(product(pair[0], pair[0]) for pair in pairs)
+    cross = sum(product(pair[0], pair[1]) for pair in pairs)
+    return main + (cross + cross.T)
+
+
+def rows_kernel(gradient, momentum, own_rows, new_momentum, held, narrow, sems):
+    loads = [
+        pltpu.make_async_copy(source, held.at[place], sems.at[place])
+        for place, source in enumerate((gradient, momentum))
+    ]
+    for load in loads:
+        load.start()
+    for load in loads:
+        load.wait()
+    value = held[0]
+    moved = momentum_mu * held[1] + value
+    narrow[...] = (value + momentum_mu * moved)[0].astype(jnp.bfloat16)
+    held[1] = moved
+    devices = own_rows.shape[0]
+    stores = [
+        pltpu.make_async_copy(narrow, own_rows.at[device], sems.at[2 + device])
+        for device in range(devices)
+    ]
+    stores.append(pltpu.make_async_copy(held.at[1], new_momentum, sems.at[2 + devices]))
+    for store in stores:
+        store.start()
+    for store in stores:
+        store.wait()
 
 
 def refit_kernel(place, count, peak, whole, master, updated, sent, held, gram_held):
     rows = master.shape[1]
     first = pl.multiple_of(place[0] * rows, rows)
-    head = whole[...]
-    current = head.astype(jnp.float32)
-    square = jnp.sum(jnp.sum(current * current, axis=0, keepdims=True), axis=1, keepdims=True)
+    width = whole.shape[1] // 2
+    blocks = [slice(block * width, (block + 1) * width) for block in range(2)]
+    head = [whole[:, block] for block in blocks]
+    current = [part.astype(jnp.float32) for part in head]
+    square = sum(
+        jnp.sum(jnp.sum(part * part, axis=0, keepdims=True), axis=1, keepdims=True)
+        for part in current
+    )
     scale = 1.0 / (jnp.sqrt(square) + epsilon)
-    gram = dot_t(head, head) * scale * scale
+    gram = sum(dot_t(part, part) for part in head) * scale * scale
     for iteration in range(ITERS - 1):
         pair = split(gram)
-        poly = split(newton_b * gram + newton_c * three_gram(pair, dot))
+        poly = split(newton_b * gram + newton_c * symmetric([pair], dot))
         if iteration == 0:
-            current = (newton_a * current + (dot(poly[0], head) + dot(poly[1], head))) * scale
+            current = [
+                (newton_a * old + (dot(poly[0], part) + dot(poly[1], part))) * scale
+                for old, part in zip(current, head)
+            ]
         else:
-            current = newton_a * current + three(dot, poly, halves)
-        halves = split(current)
-        gram = three_gram(halves, dot_t)
-    held[...] = current
+            current = [
+                newton_a * old + three(dot, poly, part) for old, part in zip(current, halves)
+            ]
+        halves = [split(part) for part in current]
+        gram = symmetric(halves, dot_t)
+    for block, part in zip(blocks, current):
+        held[:, block] = part
     gram_held[...] = gram
     gram_rows = gram_held[pl.ds(first, rows), :]
-    poly = newton_b * gram_rows + newton_c * three(dot, split(gram_rows), split(gram))
-    ortho = newton_a * held[pl.ds(first, rows), :] + three(dot, split(poly), halves)
+    poly = split(newton_b * gram_rows + newton_c * three(dot, split(gram_rows), split(gram)))
+    turned = jnp.concatenate([three(dot, poly, part) for part in halves], axis=1)
+    ortho = newton_a * held[pl.ds(first, rows), :] + turned
 
     shape = ortho.shape
     gamma = jnp.where(count[0] > 0, clip_tau / jnp.full(shape, peak[0], jnp.float32), 1.0)
@@ -133,8 +173,6 @@
 
 
 def shards(gradient, momentum, master, clip_count, logit_peak, server_map):
-    new_momentum = momentum_mu * momentum + gradient
-    nesterov = gradient + momentum_mu * new_momentum
     _, row_count, columns = gradient.shape
     shard_count = lax.axis_size(SHARD_AXIS)
     heads = server_map.shape[0]
@@ -143,7 +181,21 @@
     shard_pos = lax.axis_index(SHARD_AXIS).astype(jnp.int32)[None]
     core_pos = lax.axis_index("core").astype(jnp.int32)[None]
 
-    own_rows = jnp.broadcast_to(nesterov.astype(jnp.bfloat16), (shard_count, row_count, columns))
+    own_rows, new_momentum = pl.pallas_call(
+        rows_kernel,
+        out_shape=(
+            jax.ShapeDtypeStruct((shard_count, row_count, columns), jnp.bfloat16),
+            jax.ShapeDtypeStruct(momentum.shape, jnp.float32),
+        ),
+        in_specs=[HBM, HBM],
+        out_specs=(HBM, HBM),
+        scratch_shapes=[
+            pltpu.VMEM((2, *gradient.shape), jnp.float32),
+            pltpu.VMEM((row_count, columns), jnp.bfloat16),
+            pltpu.SemaphoreType.DMA((shard_count + 3,)),
+        ],
+        compiler_params=WHOLE,
+    )(gradient, momentum)
     whole_head = lax.all_to_all(own_rows, SHARD_AXIS, 0, 0, tiled=True)
     whole_head = whole_head.reshape(shard_count * row_count, columns)
 

time: 98.4 us -> 97.6 us (level)
  Pallas kernels: 6.98 us -> 8.45 us
  other arithmetic: 1.4 us -> 0 us
    pallas_call x0 -> x1, Pallas kernels: none -> 1.65 us  [shards(): pl.pallas_call(rows_kernel, out_shape=(jax.ShapeDtypeStruct((shard_count,...]
    broadcast_in_dim x1 -> x0, other arithmetic: 1.4 us -> none  [shards(): jnp.broadcast_to(nesterov.astype(jnp.bfloat16), (shard_count, row_count,...]
where the time goes in v6:
time: 97.6 us; the launch traced here: 97.1 us
  blocking collectives  64.5 us (66%)
  starting transfers between devices  14.1 us (14%)
  Pallas kernels  8.45 us (9%)
  waiting for transfers between devices  7.97 us (8%)
  between operations  1.98 us (2%)
    all_to_all x1, blocking collectives, shards(): head_parts = lax.all_to_all(sent, HEAD_AXES, 0, 0, tiled=True)  43.3 us
    all_to_all x1, blocking collectives, shards(): own = lax.all_to_all(ordered, SHARD_AXIS, 0, 0, tiled=True)  11.3 us
    all_to_all x1, blocking collectives, shards(): own = lax.all_to_all(own, SHARERS, 0, 0, tiled=True)  9.88 us
    all_to_all x1, starting transfers between devices, shards(): whole_head = lax.all_to_all(own_rows, SHARD_AXIS, 0, 0, tiled=True)  8.69 us
    all_to_all x1, waiting for transfers between devices, shards(): whole_head = lax.all_to_all(own_rows, SHARD_AXIS, 0, 0, tiled=True)  6.46 us
    ppermute x1, starting transfers between devices, shards(): other = lax.ppermute(own, 'core', [(0, 1), (1, 0)])  5.4 us
    pallas_call x1, Pallas kernels, shards(): pl.pallas_call(refit_kernel, out_shape=(jax.ShapeDtypeStruct(master.shape...  5.17 us
  transfers between devices with their start and end apart: 2, of which 2 were waited for; matrix products, arithmetic and copies ran while one was open for 0% of the time, Pallas kernels for 0%

profile of v6, /device:TPU:1, one launch (start us, length us, event | category | flops | bytes accessed | tf_op | source)
XLA Modules:
  0.0 97.1 jit_solution(14623551421632644368)
XLA Ops:
  0.6 1.6 %shard_map.85 = (bf16[16,16,512]{2,1,0:T(8,128)(2,1)}, f32[1,16,512]{2,1,0:T(8,128)}) custom-call(f32[1,16,512]{2,1,0:T(8,128)} %gradient.1, f32[1,16,512]{2,1,0:T(8,128)} %momentum.1), custom_call_target="tpu_custom_call" | custom-call | tf_op jit(solution)/shard_map/pallas_call | solution.py:184
  2.3 0.0 copy-start
  2.3 8.7 %all-to-all-start = ((bf16[16,16,512]{2,1,0:T(8,128)(2,1)}), bf16[16,16,512]{2,1,0:T(8,128)(2,1)S(1)}, u32[]{:S(2)}, u32[]{:S(2)}) async-start(bf16[16,16,512]{2,1,0:T(8,128)(2,1)} %get-tuple-element.7), calls=%async_computation | async-start | bytes 524288 | tf_op jit(solution)/shard_map/all_to_all | solution.py:199
  12.3 6.5 %all-to-all-done = bf16[16,16,512]{2,1,0:T(8,128)(2,1)S(1)} async-done(((bf16[16,16,512]{2,1,0:T(8,128)(2,1)}), bf16[16,16,512]{2,1,0:T(8,128)(2,1)S(1)}, u32[]{:S(2)}, u32[]{:S(2)}) %all-to-all-start) | async-done | bytes 262176 | tf_op jit(solution)/shard_map/all_to_all | solution.py:199
  18.8 0.0 copy-done
  18.8 5.2 %shard_map.86 = (f32[1,16,512]{2,1,0:T(8,128)}, bf16[64,8,128]{2,1,0:T(8,128)(2,1)S(1)}) custom-call(s32[1]{0:T(128)} %bitcast.place, s32[1]{0:T(128)S(6)} %copy.9.count, f32[1]{0:T(128)S(6)} %copy.10.peak, bf16[256,512]{1,0:T(8,128)(2,1)S(1)} %bitcast.7, f32[1,16,512]{2,1,0:T(8,128)S(1)} %copy-done), custom_call_target="tpu_custom_call" | custom-call | tf_op jit(solution)/shard_map/pallas_call | solution.py:202
  23.9 0.0 copy-start.1
  23.9 43.3 %all_to_all.20.parts = bf16[64,8,128]{2,1,0:T(8,128)(2,1)S(1)} all-to-all(bf16[64,8,128]{2,1,0:T(8,128)(2,1)S(1)} %get-tuple-element.10), channel_id=1, replica_groups=mesh['xh'=2,'zh'=8,'zl'=2,'core'=2,'shard'=16] {'xh','zh','zl','core'}, dimensions={0} | all-to-all | bytes 262144 | tf_op jit(solution)/shard_map/all_to_all | solution.py:217
  67.3 0.0 copy-done.1
  67.3 0.6 shard_map.87
  67.9 11.3 %all_to_all.21 = bf16[16,4,8,128]{3,2,1,0:T(8,128)(2,1)S(1)} all-to-all(bf16[16,4,8,128]{3,2,1,0:T(8,128)(2,1)S(1)} %bitcast.8), channel_id=1, replica_groups=mesh['xh'=2,'zh'=8,'zl'=2,'core'=2,'shard'=16] {'shard'}, dimensions={0} | all-to-all | bytes 262144 | tf_op jit(solution)/shard_map/all_to_all | solution.py:226
  79.2 0.1 broadcast_in_dim.11
  79.3 9.9 %all_to_all.22 = bf16[4,16,4,8,128]{4,3,2,1,0:T(8,128)(2,1)S(1)} all-to-all(bf16[4,16,4,8,128]{4,3,2,1,0:T(8,128)(2,1)S(1)} %broadcast_in_dim.11), channel_id=1, replica_groups=mesh['xh'=2,'zh'=8,'zl'=2,'core'=2,'shard'=16] {'xh','zl'}, dimensions={0} | all-to-all | bytes 1048576 | tf_op jit(solution)/shard_map/all_to_all | solution.py:228
  89.1 5.4 %collective-permute-start = (bf16[2,2,16,4,8,128]{5,4,3,2,1,0:T(8,128)(2,1)S(1)}, bf16[2,2,16,4,8,128]{5,4,3,2,1,0:T(8,128)(2,1)S(1)}, u32[]{:S(2)}, u32[]{:S(2)}) collective-permute-start(bf16[2,2,16,4,8,128]{5,4,3,2,1,0:T(8,128)(2,1)S(1)} %bitcast.5), channel_id=1, source_target_pairs={{0,16},{16,0},{1,17},{17,1},{2,18},{18,2},{3,19},{19,3},{4,20},{20... | collective-permute-start | bytes 1572872 | tf_op jit(solution)/shard_map/ppermute | solution.py:230
  94.5 1.5 %collective-permute-done.other = bf16[2,2,16,4,8,128]{5,4,3,2,1,0:T(8,128)(2,1)S(1)} collective-permute-done((bf16[2,2,16,4,8,128]{5,4,3,2,1,0:T(8,128)(2,1)S(1)}, bf16[2,2,16,4,8,128]{5,4,3,2,1,0:T(8,128)(2,1)S(1)}, u32[]{:S(2)}, u32[]{:S(2)}) %collective-permute-start) | collective-permute-done | bytes 524320 | tf_op jit(solution)/shard_map/ppermute | solution.py:230
  96.1 1.0 %shard_map.88 = bf16[4,256,512]{2,1,0:T(8,128)(2,1)} custom-call(s32[1]{0:T(128)} %bitcast.2.core, bf16[2,2,16,4,8,128]{5,4,3,2,1,0:T(8,128)(2,1)S(1)} %bitcast.6, bf16[2,2,16,4,8,128]{5,4,3,2,1,0:T(8,128)(2,1)S(1)} %collective-permute-done.other), custom_call_target="tpu_custom_call" | custom-call | tf_op jit(solution)/shard_map/pallas_call | solution.py:232
Async XLA Ops:
  2.3 16.5 %copy-start = (f32[1,16,512]{2,1,0:T(8,128)S(1)}, f32[1,16,512]{2,1,0:T(8,128)}, u32[]{:S(2)}) copy-start(f32[1,16,512]{2,1,0:T(8,128)} %master.1) | copy-start | bytes 98308
  2.3 16.5 %all-to-all-start = ((bf16[16,16,512]{2,1,0:T(8,128)(2,1)}), bf16[16,16,512]{2,1,0:T(8,128)(2,1)S(1)}, u32[]{:S(2)}, u32[]{:S(2)}) async-start(bf16[16,16,512]{2,1,0:T(8,128)(2,1)} %get-tuple-element.7), calls=%async_computation | async-start | bytes 524288 | tf_op jit(solution)/shard_map/all_to_all | solution.py:199
  23.9 43.3 %copy-start.1 = (s32[64]{0:T(128)S(1)}, s32[64]{0:T(128)}, u32[]{:S(2)}) copy-start(s32[64]{0:T(128)} %server_map.1) | copy-start | bytes 772
  89.1 6.9 %collective-permute-start = (bf16[2,2,16,4,8,128]{5,4,3,2,1,0:T(8,128)(2,1)S(1)}, bf16[2,2,16,4,8,128]{5,4,3,2,1,0:T(8,128)(2,1)S(1)}, u32[]{:S(2)}, u32[]{:S(2)}) collective-permute-start(bf16[2,2,16,4,8,128]{5,4,3,2,1,0:T(8,128)(2,1)S(1)} %bitcast.5), channel_id=1, source_target_pairs={{0,16},{16,0},{1,17},{17,1},{2,18},{18,2},{3,19},{19,3},{4,20},{20... | collective-permute-start | bytes 1572872 | tf_op jit(solution)/shard_map/ppermute | solution.py:230

commit v7 on v6

--- a/solution.py
+++ b/solution.py
@@ -139,7 +139,9 @@
 
 def order_kernel(server_map, parts, ordered):
     for slot in range(parts.shape[0]):
-        ordered[slot] = parts[server_map[slot]]
+        part = parts[server_map[slot]]
+        for sharer in range(ordered.shape[0]):
+            ordered[sharer, slot] = part
 
 
 def join_kernel(core, own, other, serving, held, sems):
@@ -215,17 +217,16 @@
     )(shard_pos, clip_count, logit_peak, whole_head, master)
 
     head_parts = lax.all_to_all(sent, HEAD_AXES, 0, 0, tiled=True)
+    sharers = lax.axis_size(SHARERS)
     ordered = pl.pallas_call(
         order_kernel,
-        out_shape=jax.ShapeDtypeStruct(head_parts.shape, jnp.bfloat16),
+        out_shape=jax.ShapeDtypeStruct((sharers, *head_parts.shape), jnp.bfloat16),
         in_specs=[SMEM, VMEM],
         out_specs=VMEM,
         compiler_params=SMALL,
     )(server_map, head_parts)
-    ordered = ordered.reshape(shard_count, slots, height, width)
-    own = lax.all_to_all(ordered, SHARD_AXIS, 0, 0, tiled=True)
-    own = jnp.broadcast_to(own, (PARTS, *own.shape))
-    own = lax.all_to_all(own, SHARERS, 0, 0, tiled=True)
+    ordered = ordered.reshape(sharers * shard_count, slots, height, width)
+    own = lax.all_to_all(ordered, (*SHARERS, SHARD_AXIS), 0, 0, tiled=True)
     own = own.reshape(2, 2, shard_count, slots, height, width)
     other = lax.ppermute(own, "core", [(0, 1), (1, 0)])
     serving_shape = (slots, shard_count * row_count, columns)

time: 97.6 us -> 96.9 us (level)
    all_to_all x2 -> x1, blocking collectives: 21.2 us -> 21.2 us  [shards(): own = lax.all_to_all(ordered, (*SHARERS, SHARD_AXIS), 0, 0, tiled=True)]
where the time goes in v7:
time: 96.9 us; the launch traced here: 96.5 us
  blocking collectives  64.5 us (67%)
  starting transfers between devices  13.5 us (14%)
  Pallas kernels  8.47 us (9%)
  waiting for transfers between devices  7.97 us (8%)
  between operations  1.98 us (2%)
    all_to_all x1, blocking collectives, shards(): head_parts = lax.all_to_all(sent, HEAD_AXES, 0, 0, tiled=True)  43.3 us
    all_to_all x1, blocking collectives, shards(): own = lax.all_to_all(ordered, (*SHARERS, SHARD_AXIS), 0, 0, tiled=True)  21.2 us
    all_to_all x1, starting transfers between devices, shards(): whole_head = lax.all_to_all(own_rows, SHARD_AXIS, 0, 0, tiled=True)  8.69 us
    all_to_all x1, waiting for transfers between devices, shards(): whole_head = lax.all_to_all(own_rows, SHARD_AXIS, 0, 0, tiled=True)  6.46 us
    pallas_call x1, Pallas kernels, shards(): pl.pallas_call(refit_kernel, out_shape=(jax.ShapeDtypeStruct(master.shape...  5.17 us
    ppermute x1, starting transfers between devices, shards(): other = lax.ppermute(own, 'core', [(0, 1), (1, 0)])  4.83 us
  transfers between devices with their start and end apart: 2, of which 2 were waited for; matrix products, arithmetic and copies ran while one was open for 0% of the time, Pallas kernels for 0%

profile of v7, /device:TPU:1, one launch (start us, length us, event | category | flops | bytes accessed | tf_op | source)
XLA Modules:
  0.0 96.5 jit_solution(14132857126699040410)
XLA Ops:
  0.6 1.6 %shard_map.85 = (bf16[16,16,512]{2,1,0:T(8,128)(2,1)}, f32[1,16,512]{2,1,0:T(8,128)}) custom-call(f32[1,16,512]{2,1,0:T(8,128)} %gradient.1, f32[1,16,512]{2,1,0:T(8,128)} %momentum.1), custom_call_target="tpu_custom_call" | custom-call | tf_op jit(solution)/shard_map/pallas_call | solution.py:186
  2.3 0.0 copy-start
  2.3 8.7 %all-to-all-start = ((bf16[16,16,512]{2,1,0:T(8,128)(2,1)}), bf16[16,16,512]{2,1,0:T(8,128)(2,1)S(1)}, u32[]{:S(2)}, u32[]{:S(2)}) async-start(bf16[16,16,512]{2,1,0:T(8,128)(2,1)} %get-tuple-element.7), calls=%async_computation | async-start | bytes 524288 | tf_op jit(solution)/shard_map/all_to_all | solution.py:201
  12.3 6.5 %all-to-all-done = bf16[16,16,512]{2,1,0:T(8,128)(2,1)S(1)} async-done(((bf16[16,16,512]{2,1,0:T(8,128)(2,1)}), bf16[16,16,512]{2,1,0:T(8,128)(2,1)S(1)}, u32[]{:S(2)}, u32[]{:S(2)}) %all-to-all-start) | async-done | bytes 262176 | tf_op jit(solution)/shard_map/all_to_all | solution.py:201
  18.8 0.0 copy-done
  18.8 5.2 %shard_map.86 = (f32[1,16,512]{2,1,0:T(8,128)}, bf16[64,8,128]{2,1,0:T(8,128)(2,1)S(1)}) custom-call(s32[1]{0:T(128)} %bitcast.place, s32[1]{0:T(128)S(6)} %copy.9.count, f32[1]{0:T(128)S(6)} %copy.10.peak, bf16[256,512]{1,0:T(8,128)(2,1)S(1)} %bitcast.8, f32[1,16,512]{2,1,0:T(8,128)S(1)} %copy-done), custom_call_target="tpu_custom_call" | custom-call | tf_op jit(solution)/shard_map/pallas_call | solution.py:204
  23.9 0.0 copy-start.1
  23.9 43.3 %all_to_all.15.parts = bf16[64,8,128]{2,1,0:T(8,128)(2,1)S(1)} all-to-all(bf16[64,8,128]{2,1,0:T(8,128)(2,1)S(1)} %get-tuple-element.10), channel_id=1, replica_groups=mesh['xh'=2,'zh'=8,'zl'=2,'core'=2,'shard'=16] {'xh','zh','zl','core'}, dimensions={0} | all-to-all | bytes 262144 | tf_op jit(solution)/shard_map/all_to_all | solution.py:219
  67.3 0.0 copy-done.1
  67.3 0.6 shard_map.87
  67.9 21.2 %all_to_all.16 = bf16[64,4,8,128]{3,2,1,0:T(8,128)(2,1)S(1)} all-to-all(bf16[64,4,8,128]{3,2,1,0:T(8,128)(2,1)S(1)} %bitcast.7), channel_id=1, replica_groups=mesh['xh'=2,'zh'=8,'zl'=2,'core'=2,'shard'=16] {'xh','zl','shard'}, dimensions={0} | all-to-all | bytes 1048576 | tf_op jit(solution)/shard_map/all_to_all | solution.py:229
  89.1 4.8 %collective-permute-start = (bf16[2,2,16,4,8,128]{5,4,3,2,1,0:T(8,128)(2,1)S(1)}, bf16[2,2,16,4,8,128]{5,4,3,2,1,0:T(8,128)(2,1)S(1)}, u32[]{:S(2)}, u32[]{:S(2)}) collective-permute-start(bf16[2,2,16,4,8,128]{5,4,3,2,1,0:T(8,128)(2,1)S(1)} %bitcast.5), channel_id=1, source_target_pairs={{0,16},{16,0},{1,17},{17,1},{2,18},{18,2},{3,19},{19,3},{4,20},{20... | collective-permute-start | bytes 1572872 | tf_op jit(solution)/shard_map/ppermute | solution.py:231
  93.9 1.5 %collective-permute-done.other = bf16[2,2,16,4,8,128]{5,4,3,2,1,0:T(8,128)(2,1)S(1)} collective-permute-done((bf16[2,2,16,4,8,128]{5,4,3,2,1,0:T(8,128)(2,1)S(1)}, bf16[2,2,16,4,8,128]{5,4,3,2,1,0:T(8,128)(2,1)S(1)}, u32[]{:S(2)}, u32[]{:S(2)}) %collective-permute-start) | collective-permute-done | bytes 524320 | tf_op jit(solution)/shard_map/ppermute | solution.py:231
  95.4 1.0 %shard_map.88 = bf16[4,256,512]{2,1,0:T(8,128)(2,1)} custom-call(s32[1]{0:T(128)} %bitcast.2.core, bf16[2,2,16,4,8,128]{5,4,3,2,1,0:T(8,128)(2,1)S(1)} %bitcast.6, bf16[2,2,16,4,8,128]{5,4,3,2,1,0:T(8,128)(2,1)S(1)} %collective-permute-done.other), custom_call_target="tpu_custom_call" | custom-call | tf_op jit(solution)/shard_map/pallas_call | solution.py:233
Async XLA Ops:
  2.3 16.5 %copy-start = (f32[1,16,512]{2,1,0:T(8,128)S(1)}, f32[1,16,512]{2,1,0:T(8,128)}, u32[]{:S(2)}) copy-start(f32[1,16,512]{2,1,0:T(8,128)} %master.1) | copy-start | bytes 98308
  2.3 16.5 %all-to-all-start = ((bf16[16,16,512]{2,1,0:T(8,128)(2,1)}), bf16[16,16,512]{2,1,0:T(8,128)(2,1)S(1)}, u32[]{:S(2)}, u32[]{:S(2)}) async-start(bf16[16,16,512]{2,1,0:T(8,128)(2,1)} %get-tuple-element.7), calls=%async_computation | async-start | bytes 524288 | tf_op jit(solution)/shard_map/all_to_all | solution.py:201
  23.9 43.3 %copy-start.1 = (s32[64]{0:T(128)S(1)}, s32[64]{0:T(128)}, u32[]{:S(2)}) copy-start(s32[64]{0:T(128)} %server_map.1) | copy-start | bytes 772
  89.1 6.4 %collective-permute-start = (bf16[2,2,16,4,8,128]{5,4,3,2,1,0:T(8,128)(2,1)S(1)}, bf16[2,2,16,4,8,128]{5,4,3,2,1,0:T(8,128)(2,1)S(1)}, u32[]{:S(2)}, u32[]{:S(2)}) collective-permute-start(bf16[2,2,16,4,8,128]{5,4,3,2,1,0:T(8,128)(2,1)S(1)} %bitcast.5), channel_id=1, source_target_pairs={{0,16},{16,0},{1,17},{17,1},{2,18},{18,2},{3,19},{19,3},{4,20},{20... | collective-permute-start | bytes 1572872 | tf_op jit(solution)/shard_map/ppermute | solution.py:231

commit v8 on v7

--- a/solution.py
+++ b/solution.py
@@ -144,34 +144,38 @@
             ordered[sharer, slot] = part
 
 
-def join_kernel(core, own, other, serving, held, sems):
-    sides, _, blocks, slots, height, width = own.shape
+def fill_half(half, source, serving, held, sems):
+    sides, _, blocks, slots, height, width = source.shape
     rows = 2 * height
-
-    def fill(slot, lower, upper):
-        for half, source in enumerate((lower, upper)):
-            for side in range(sides):
-                part = half * sides + side
-                for block in range(blocks):
-                    held[
-                        slot, block * rows : (block + 1) * rows, part * width : (part + 1) * width
-                    ] = jnp.concatenate(
-                        [source[side, 0, block, slot], source[side, 1, block, slot]], axis=0
-                    )
-
+    first = pl.multiple_of(half * (sides * width), sides * width)
+    copies = []
     for slot in range(slots):
-
-        @pl.when(core[0] == 0)
-        def _():
-            fill(slot, own, other)
-
-        @pl.when(core[0] != 0)
-        def _():
-            fill(slot, other, own)
-
-        pltpu.make_async_copy(held.at[slot], serving.at[slot], sems.at[slot]).start()
-    for slot in range(slots):
-        pltpu.make_async_copy(held.at[slot], serving.at[slot], sems.at[slot]).wait()
+        for side in range(sides):
+            for block in range(blocks):
+                held[
+                    slot, block * rows : (block + 1) * rows, side * width : (side + 1) * width
+                ] = jnp.concatenate(
+                    [source[side, 0, block, slot], source[side, 1, block, slot]], axis=0
+                )
+        copies.append(
+            pltpu.make_async_copy(
+                held.at[slot], serving.at[slot, :, pl.ds(first, sides * width)], sems.at[slot]
+            )
+        )
+        copies[-1].start()
+    for copy in copies:
+        copy.wait()
+
+
+def own_kernel(core, own, serving, held, sems):
+    fill_half(core[0], own, serving, held, sems)
+
+
+def other_kernel(core, other, updated, half_done, serving, new_master, held, sems):
+    master_copy = pltpu.make_async_copy(updated, new_master, sems.at[other.shape[3]])
+    master_copy.start()
+    fill_half(1 - core[0], other, serving, held, sems)
+    master_copy.wait()
 
 
 def shards(gradient, momentum, master, clip_count, logit_peak, server_map):
@@ -229,19 +233,31 @@
     own = lax.all_to_all(ordered, (*SHARERS, SHARD_AXIS), 0, 0, tiled=True)
     own = own.reshape(2, 2, shard_count, slots, height, width)
     other = lax.ppermute(own, "core", [(0, 1), (1, 0)])
-    serving_shape = (slots, shard_count * row_count, columns)
+    serving_shape = jax.ShapeDtypeStruct(
+        (slots, shard_count * row_count, columns), jnp.bfloat16
+    )
+    scratch = [
+        pltpu.VMEM((slots, shard_count * row_count, columns // 2), jnp.bfloat16),
+        pltpu.SemaphoreType.DMA((slots + 1,)),
+    ]
     serving = pl.pallas_call(
-        join_kernel,
-        out_shape=jax.ShapeDtypeStruct(serving_shape, jnp.bfloat16),
-        in_specs=[SMEM, VMEM, VMEM],
-        out_specs=pl.BlockSpec(memory_space=pl.ANY),
-        scratch_shapes=[
-            pltpu.VMEM(serving_shape, jnp.bfloat16),
-            pltpu.SemaphoreType.DMA((slots,)),
-        ],
+        own_kernel,
+        out_shape=serving_shape,
+        in_specs=[SMEM, VMEM],
+        out_specs=HBM,
+        scratch_shapes=scratch,
         compiler_params=SMALL,
-    )(core_pos, own, other)
-    return (updated, new_momentum, serving)
+    )(core_pos, own)
+    serving, new_master = pl.pallas_call(
+        other_kernel,
+        out_shape=(serving_shape, jax.ShapeDtypeStruct(updated.shape, jnp.float32)),
+        in_specs=[SMEM, VMEM, VMEM, HBM],
+        out_specs=(HBM, HBM),
+        scratch_shapes=scratch,
+        input_output_aliases={3: 0},
+        compiler_params=SMALL,
+    )(core_pos, other, updated, serving)
+    return (new_master, new_momentum, serving)
 
 
 def solution(mesh):

time: 96.9 us -> 96 us (level)
  transfers between devices with their start and end apart: 2 -> 2, of which waited for: 2 -> 2; matrix products, arithmetic and copies ran while one was open for 0% -> 0% of each run, Pallas kernels for 0% -> 1%
where the time goes in v8:
time: 96 us; the launch traced here: 95.6 us
  blocking collectives  64.4 us (67%)
  starting transfers between devices  13.5 us (14%)
  Pallas kernels  8.52 us (9%)
  waiting for transfers between devices  7.11 us (7%)
  between operations  2 us (2%)
    all_to_all x1, blocking collectives, shards(): head_parts = lax.all_to_all(sent, HEAD_AXES, 0, 0, tiled=True)  43.2 us
    all_to_all x1, blocking collectives, shards(): own = lax.all_to_all(ordered, (*SHARERS, SHARD_AXIS), 0, 0, tiled=True)  21.2 us
    all_to_all x1, starting transfers between devices, shards(): whole_head = lax.all_to_all(own_rows, SHARD_AXIS, 0, 0, tiled=True)  8.69 us
    all_to_all x1, waiting for transfers between devices, shards(): whole_head = lax.all_to_all(own_rows, SHARD_AXIS, 0, 0, tiled=True)  6.46 us
    ppermute x1, starting transfers between devices, shards(): other = lax.ppermute(own, 'core', [(0, 1), (1, 0)])  4.83 us
    pallas_call x1, Pallas kernels, shards(): pl.pallas_call(refit_kernel, out_shape=(jax.ShapeDtypeStruct(master.shape...  4.55 us
  transfers between devices with their start and end apart: 2, of which 2 were waited for; matrix products, arithmetic and copies ran while one was open for 0% of the time, Pallas kernels for 1%

profile of v8, /device:TPU:1, one launch (start us, length us, event | category | flops | bytes accessed | tf_op | source)
XLA Modules:
  0.0 95.6 jit_solution(17934644908415060118)
XLA Ops:
  0.6 1.6 %shard_map.85 = (bf16[16,16,512]{2,1,0:T(8,128)(2,1)}, f32[1,16,512]{2,1,0:T(8,128)}) custom-call(f32[1,16,512]{2,1,0:T(8,128)} %gradient.1, f32[1,16,512]{2,1,0:T(8,128)} %momentum.1), custom_call_target="tpu_custom_call" | custom-call | tf_op jit(solution)/shard_map/pallas_call | solution.py:190
  2.3 0.0 copy-start
  2.3 8.7 %all-to-all-start = ((bf16[16,16,512]{2,1,0:T(8,128)(2,1)}), bf16[16,16,512]{2,1,0:T(8,128)(2,1)S(1)}, u32[]{:S(2)}, u32[]{:S(2)}) async-start(bf16[16,16,512]{2,1,0:T(8,128)(2,1)} %get-tuple-element.9), calls=%async_computation | async-start | bytes 524288 | tf_op jit(solution)/shard_map/all_to_all | solution.py:205
  12.3 6.5 %all-to-all-done = bf16[16,16,512]{2,1,0:T(8,128)(2,1)S(1)} async-done(((bf16[16,16,512]{2,1,0:T(8,128)(2,1)}), bf16[16,16,512]{2,1,0:T(8,128)(2,1)S(1)}, u32[]{:S(2)}, u32[]{:S(2)}) %all-to-all-start) | async-done | bytes 262176 | tf_op jit(solution)/shard_map/all_to_all | solution.py:205
  18.8 0.0 copy-done
  18.8 4.6 %shard_map.86 = (f32[1,16,512]{2,1,0:T(8,128)S(1)}, bf16[64,8,128]{2,1,0:T(8,128)(2,1)S(1)}) custom-call(s32[1]{0:T(128)} %bitcast.1.place, s32[1]{0:T(128)S(6)} %copy.11.count, f32[1]{0:T(128)S(6)} %copy.12.peak, bf16[256,512]{1,0:T(8,128)(2,1)S(1)} %bitcast.8, f32[1,16,512]{2,1,0:T(8,128)S(1)} %copy-done), custom_call_target="tpu_custom_call" | custom-call | tf_op jit(solution)/shard_map/pallas_call | solution.py:208
  23.3 0.0 copy-start.1
  23.3 43.2 %all_to_all.15.parts = bf16[64,8,128]{2,1,0:T(8,128)(2,1)S(1)} all-to-all(bf16[64,8,128]{2,1,0:T(8,128)(2,1)S(1)} %get-tuple-element.10), channel_id=1, replica_groups=mesh['xh'=2,'zh'=8,'zl'=2,'core'=2,'shard'=16] {'xh','zh','zl','core'}, dimensions={0} | all-to-all | bytes 262144 | tf_op jit(solution)/shard_map/all_to_all | solution.py:223
  66.6 0.0 copy-done.1
  66.6 0.6 shard_map.87
  67.2 21.2 %all_to_all.16 = bf16[64,4,8,128]{3,2,1,0:T(8,128)(2,1)S(1)} all-to-all(bf16[64,4,8,128]{3,2,1,0:T(8,128)(2,1)S(1)} %bitcast.7), channel_id=1, replica_groups=mesh['xh'=2,'zh'=8,'zl'=2,'core'=2,'shard'=16] {'xh','zl','shard'}, dimensions={0} | all-to-all | bytes 1048576 | tf_op jit(solution)/shard_map/all_to_all | solution.py:233
  88.4 4.8 %collective-permute-start = (bf16[2,2,16,4,8,128]{5,4,3,2,1,0:T(8,128)(2,1)S(1)}, bf16[2,2,16,4,8,128]{5,4,3,2,1,0:T(8,128)(2,1)S(1)}, u32[]{:S(2)}, u32[]{:S(2)}) collective-permute-start(bf16[2,2,16,4,8,128]{5,4,3,2,1,0:T(8,128)(2,1)S(1)} %bitcast.5), channel_id=1, source_target_pairs={{0,16},{16,0},{1,17},{17,1},{2,18},{18,2},{3,19},{19,3},{4,20},{20... | collective-permute-start | bytes 1572872 | tf_op jit(solution)/shard_map/ppermute | solution.py:235
  93.2 0.9 shard_map.88.half_done
  94.1 0.6 collective-permute-done.other
  94.7 0.9 shard_map.89
Async XLA Ops:
  2.3 16.5 %copy-start = (f32[1,16,512]{2,1,0:T(8,128)S(1)}, f32[1,16,512]{2,1,0:T(8,128)}, u32[]{:S(2)}) copy-start(f32[1,16,512]{2,1,0:T(8,128)} %master.1) | copy-start | bytes 98308
  2.3 16.5 %all-to-all-start = ((bf16[16,16,512]{2,1,0:T(8,128)(2,1)}), bf16[16,16,512]{2,1,0:T(8,128)(2,1)S(1)}, u32[]{:S(2)}, u32[]{:S(2)}) async-start(bf16[16,16,512]{2,1,0:T(8,128)(2,1)} %get-tuple-element.9), calls=%async_computation | async-start | bytes 524288 | tf_op jit(solution)/shard_map/all_to_all | solution.py:205
  23.3 43.2 %copy-start.1 = (s32[64]{0:T(128)S(1)}, s32[64]{0:T(128)}, u32[]{:S(2)}) copy-start(s32[64]{0:T(128)} %server_map.1) | copy-start | bytes 772
  88.4 6.4 %collective-permute-start = (bf16[2,2,16,4,8,128]{5,4,3,2,1,0:T(8,128)(2,1)S(1)}, bf16[2,2,16,4,8,128]{5,4,3,2,1,0:T(8,128)(2,1)S(1)}, u32[]{:S(2)}, u32[]{:S(2)}) collective-permute-start(bf16[2,2,16,4,8,128]{5,4,3,2,1,0:T(8,128)(2,1)S(1)} %bitcast.5), channel_id=1, source_target_pairs={{0,16},{16,0},{1,17},{17,1},{2,18},{18,2},{3,19},{19,3},{4,20},{20... | collective-permute-start | bytes 1572872 | tf_op jit(solution)/shard_map/ppermute | solution.py:235

commit v9 on v8

--- a/solution.py
+++ b/solution.py
@@ -85,9 +85,9 @@
         store.wait()
 
 
-def refit_kernel(place, count, peak, whole, master, updated, sent, held, gram_held):
+def refit_kernel(count, peak, whole, master, updated, sent, held, gram_held):
     rows = master.shape[1]
-    first = pl.multiple_of(place[0] * rows, rows)
+    first = pl.multiple_of(lax.axis_index(SHARD_AXIS) * rows, rows)
     width = whole.shape[1] // 2
     blocks = [slice(block * width, (block + 1) * width) for block in range(2)]
     head = [whole[:, block] for block in blocks]
@@ -167,14 +167,14 @@
         copy.wait()
 
 
-def own_kernel(core, own, serving, held, sems):
-    fill_half(core[0], own, serving, held, sems)
-
-
-def other_kernel(core, other, updated, half_done, serving, new_master, held, sems):
+def own_kernel(own, serving, held, sems):
+    fill_half(lax.axis_index("core"), own, serving, held, sems)
+
+
+def other_kernel(other, updated, half_done, serving, new_master, held, sems):
     master_copy = pltpu.make_async_copy(updated, new_master, sems.at[other.shape[3]])
     master_copy.start()
-    fill_half(1 - core[0], other, serving, held, sems)
+    fill_half(1 - lax.axis_index("core"), other, serving, held, sems)
     master_copy.wait()
 
 
@@ -184,8 +184,6 @@
     heads = server_map.shape[0]
     slots = heads // shard_count
     width, height = columns // PARTS, row_count // 2
-    shard_pos = lax.axis_index(SHARD_AXIS).astype(jnp.int32)[None]
-    core_pos = lax.axis_index("core").astype(jnp.int32)[None]
 
     own_rows, new_momentum = pl.pallas_call(
         rows_kernel,
@@ -211,14 +209,14 @@
             jax.ShapeDtypeStruct(master.shape, jnp.float32),
             jax.ShapeDtypeStruct((heads, height, width), jnp.bfloat16),
         ),
-        in_specs=[SMEM, SMEM, SMEM, VMEM, VMEM],
+        in_specs=[SMEM, SMEM, VMEM, VMEM],
         out_specs=(VMEM, VMEM),
         scratch_shapes=[
             pltpu.VMEM(whole_head.shape, jnp.float32),
             pltpu.VMEM((whole_head.shape[0],) * 2, jnp.float32),
         ],
         compiler_params=LARGE,
-    )(shard_pos, clip_count, logit_peak, whole_head, master)
+    )(clip_count, logit_peak, whole_head, master)
 
     head_parts = lax.all_to_all(sent, HEAD_AXES, 0, 0, tiled=True)
     sharers = lax.axis_size(SHARERS)
@@ -243,20 +241,20 @@
     serving = pl.pallas_call(
         own_kernel,
         out_shape=serving_shape,
-        in_specs=[SMEM, VMEM],
+        in_specs=[VMEM],
         out_specs=HBM,
         scratch_shapes=scratch,
         compiler_params=SMALL,
-    )(core_pos, own)
+    )(own)
     serving, new_master = pl.pallas_call(
         other_kernel,
         out_shape=(serving_shape, jax.ShapeDtypeStruct(updated.shape, jnp.float32)),
-        in_specs=[SMEM, VMEM, VMEM, HBM],
+        in_specs=[VMEM, VMEM, HBM],
         out_specs=(HBM, HBM),
         scratch_shapes=scratch,
-        input_output_aliases={3: 0},
+        input_output_aliases={2: 0},
         compiler_params=SMALL,
-    )(core_pos, other, updated, serving)
+    )(other, updated, serving)
     return (new_master, new_momentum, serving)
 
 

time: 96 us -> 96 us (level)
  no operation moved by 1% of the time
where the time goes in v9:
time: 96 us; the launch traced here: 95.6 us
  blocking collectives  64.4 us (67%)
  starting transfers between devices  13.5 us (14%)
  Pallas kernels  8.53 us (9%)
  waiting for transfers between devices  7.11 us (7%)
  between operations  1.99 us (2%)
    all_to_all x1, blocking collectives, shards(): head_parts = lax.all_to_all(sent, HEAD_AXES, 0, 0, tiled=True)  43.2 us
    all_to_all x1, blocking collectives, shards(): own = lax.all_to_all(ordered, (*SHARERS, SHARD_AXIS), 0, 0, tiled=True)  21.2 us
    all_to_all x1, starting transfers between devices, shards(): whole_head = lax.all_to_all(own_rows, SHARD_AXIS, 0, 0, tiled=True)  8.69 us
    all_to_all x1, waiting for transfers between devices, shards(): whole_head = lax.all_to_all(own_rows, SHARD_AXIS, 0, 0, tiled=True)  6.47 us
    ppermute x1, starting transfers between devices, shards(): other = lax.ppermute(own, 'core', [(0, 1), (1, 0)])  4.83 us
    pallas_call x1, Pallas kernels, shards(): pl.pallas_call(refit_kernel, out_shape=(jax.ShapeDtypeStruct(master.shape...  4.55 us
  transfers between devices with their start and end apart: 2, of which 2 were waited for; matrix products, arithmetic and copies ran while one was open for 0% of the time, Pallas kernels for 1%

profile of v9, /device:TPU:1, one launch (start us, length us, event | category | flops | bytes accessed | tf_op | source)
XLA Modules:
  0.0 95.6 jit_solution(13996243630929731007)
XLA Ops:
  0.6 1.6 %shard_map.85 = (bf16[16,16,512]{2,1,0:T(8,128)(2,1)}, f32[1,16,512]{2,1,0:T(8,128)}) custom-call(f32[1,16,512]{2,1,0:T(8,128)} %gradient.1, f32[1,16,512]{2,1,0:T(8,128)} %momentum.1), custom_call_target="tpu_custom_call" | custom-call | tf_op jit(solution)/shard_map/pallas_call | solution.py:188
  2.3 0.0 copy-start
  2.3 8.7 %all-to-all-start = ((bf16[16,16,512]{2,1,0:T(8,128)(2,1)}), bf16[16,16,512]{2,1,0:T(8,128)(2,1)S(1)}, u32[]{:S(2)}, u32[]{:S(2)}) async-start(bf16[16,16,512]{2,1,0:T(8,128)(2,1)} %get-tuple-element.9), calls=%async_computation | async-start | bytes 524288 | tf_op jit(solution)/shard_map/all_to_all | solution.py:203
  12.3 6.5 %all-to-all-done = bf16[16,16,512]{2,1,0:T(8,128)(2,1)S(1)} async-done(((bf16[16,16,512]{2,1,0:T(8,128)(2,1)}), bf16[16,16,512]{2,1,0:T(8,128)(2,1)S(1)}, u32[]{:S(2)}, u32[]{:S(2)}) %all-to-all-start) | async-done | bytes 262176 | tf_op jit(solution)/shard_map/all_to_all | solution.py:203
  18.8 0.0 copy-done
  18.8 4.6 %shard_map.86 = (f32[1,16,512]{2,1,0:T(8,128)S(1)}, bf16[64,8,128]{2,1,0:T(8,128)(2,1)S(1)}) custom-call(s32[1]{0:T(128)S(6)} %copy.11.count, f32[1]{0:T(128)S(6)} %copy.12.peak, bf16[256,512]{1,0:T(8,128)(2,1)S(1)} %bitcast.6, f32[1,16,512]{2,1,0:T(8,128)S(1)} %copy-done), custom_call_target="tpu_custom_call" | custom-call | tf_op jit(solution)/shard_map/pallas_call | solution.py:206
  23.3 0.0 copy-start.1
  23.3 43.2 %all_to_all.15.parts = bf16[64,8,128]{2,1,0:T(8,128)(2,1)S(1)} all-to-all(bf16[64,8,128]{2,1,0:T(8,128)(2,1)S(1)} %get-tuple-element.10), channel_id=1, replica_groups=mesh['xh'=2,'zh'=8,'zl'=2,'core'=2,'shard'=16] {'xh','zh','zl','core'}, dimensions={0} | all-to-all | bytes 262144 | tf_op jit(solution)/shard_map/all_to_all | solution.py:221
  66.6 0.0 copy-done.1
  66.6 0.6 shard_map.87
  67.2 21.2 %all_to_all.16 = bf16[64,4,8,128]{3,2,1,0:T(8,128)(2,1)S(1)} all-to-all(bf16[64,4,8,128]{3,2,1,0:T(8,128)(2,1)S(1)} %bitcast.5), channel_id=1, replica_groups=mesh['xh'=2,'zh'=8,'zl'=2,'core'=2,'shard'=16] {'xh','zl','shard'}, dimensions={0} | all-to-all | bytes 1048576 | tf_op jit(solution)/shard_map/all_to_all | solution.py:231
  88.4 4.8 %collective-permute-start = (bf16[2,2,16,4,8,128]{5,4,3,2,1,0:T(8,128)(2,1)S(1)}, bf16[2,2,16,4,8,128]{5,4,3,2,1,0:T(8,128)(2,1)S(1)}, u32[]{:S(2)}, u32[]{:S(2)}) collective-permute-start(bf16[2,2,16,4,8,128]{5,4,3,2,1,0:T(8,128)(2,1)S(1)} %bitcast.3), channel_id=1, source_target_pairs={{0,16},{16,0},{1,17},{17,1},{2,18},{18,2},{3,19},{19,3},{4,20},{20... | collective-permute-start | bytes 1572872 | tf_op jit(solution)/shard_map/ppermute | solution.py:233
  93.2 0.9 shard_map.88.half_done
  94.1 0.6 collective-permute-done.other
  94.7 0.9 shard_map.89
Async XLA Ops:
  2.3 16.5 %copy-start = (f32[1,16,512]{2,1,0:T(8,128)S(1)}, f32[1,16,512]{2,1,0:T(8,128)}, u32[]{:S(2)}) copy-start(f32[1,16,512]{2,1,0:T(8,128)} %master.1) | copy-start | bytes 98308
  2.3 16.5 %all-to-all-start = ((bf16[16,16,512]{2,1,0:T(8,128)(2,1)}), bf16[16,16,512]{2,1,0:T(8,128)(2,1)S(1)}, u32[]{:S(2)}, u32[]{:S(2)}) async-start(bf16[16,16,512]{2,1,0:T(8,128)(2,1)} %get-tuple-element.9), calls=%async_computation | async-start | bytes 524288 | tf_op jit(solution)/shard_map/all_to_all | solution.py:203
  23.3 43.2 %copy-start.1 = (s32[64]{0:T(128)S(1)}, s32[64]{0:T(128)}, u32[]{:S(2)}) copy-start(s32[64]{0:T(128)} %server_map.1) | copy-start | bytes 772
  88.4 6.4 %collective-permute-start = (bf16[2,2,16,4,8,128]{5,4,3,2,1,0:T(8,128)(2,1)S(1)}, bf16[2,2,16,4,8,128]{5,4,3,2,1,0:T(8,128)(2,1)S(1)}, u32[]{:S(2)}, u32[]{:S(2)}) collective-permute-start(bf16[2,2,16,4,8,128]{5,4,3,2,1,0:T(8,128)(2,1)S(1)} %bitcast.3), channel_id=1, source_target_pairs={{0,16},{16,0},{1,17},{17,1},{2,18},{18,2},{3,19},{19,3},{4,20},{20... | collective-permute-start | bytes 1572872 | tf_op jit(solution)/shard_map/ppermute | solution.py:233

commit v10 on v9

--- a/solution.py
+++ b/solution.py
@@ -167,15 +167,15 @@
         copy.wait()
 
 
-def own_kernel(own, serving, held, sems):
+def own_kernel(own, updated, serving, new_master, held, sems):
+    master_copy = pltpu.make_async_copy(updated, new_master, sems.at[own.shape[3]])
+    master_copy.start()
     fill_half(lax.axis_index("core"), own, serving, held, sems)
-
-
-def other_kernel(other, updated, half_done, serving, new_master, held, sems):
-    master_copy = pltpu.make_async_copy(updated, new_master, sems.at[other.shape[3]])
-    master_copy.start()
+    master_copy.wait()
+
+
+def other_kernel(other, half_done, serving, held, sems):
     fill_half(1 - lax.axis_index("core"), other, serving, held, sems)
-    master_copy.wait()
 
 
 def shards(gradient, momentum, master, clip_count, logit_peak, server_map):
@@ -238,23 +238,23 @@
         pltpu.VMEM((slots, shard_count * row_count, columns // 2), jnp.bfloat16),
         pltpu.SemaphoreType.DMA((slots + 1,)),
     ]
+    serving, new_master = pl.pallas_call(
+        own_kernel,
+        out_shape=(serving_shape, jax.ShapeDtypeStruct(updated.shape, jnp.float32)),
+        in_specs=[VMEM, VMEM],
+        out_specs=(HBM, HBM),
+        scratch_shapes=scratch,
+        compiler_params=SMALL,
+    )(own, updated)
     serving = pl.pallas_call(
-        own_kernel,
+        other_kernel,
         out_shape=serving_shape,
-        in_specs=[VMEM],
+        in_specs=[VMEM, HBM],
         out_specs=HBM,
         scratch_shapes=scratch,
+        input_output_aliases={1: 0},
         compiler_params=SMALL,
-    )(own)
-    serving, new_master = pl.pallas_call(
-        other_kernel,
-        out_shape=(serving_shape, jax.ShapeDtypeStruct(updated.shape, jnp.float32)),
-        in_specs=[VMEM, VMEM, HBM],
-        out_specs=(HBM, HBM),
-        scratch_shapes=scratch,
-        input_output_aliases={2: 0},
-        compiler_params=SMALL,
-    )(other, updated, serving)
+    )(other, serving)
     return (new_master, new_momentum, serving)
 
 

time: 96 us -> 96 us (level)
  no operation moved by 1% of the time
where the time goes in v10:
time: 96 us; the launch traced here: 95.6 us
  blocking collectives  64.4 us (67%)
  starting transfers between devices  13.5 us (14%)
  Pallas kernels  8.53 us (9%)
  waiting for transfers between devices  7.11 us (7%)
  between operations  1.99 us (2%)
    all_to_all x1, blocking collectives, shards(): head_parts = lax.all_to_all(sent, HEAD_AXES, 0, 0, tiled=True)  43.2 us
    all_to_all x1, blocking collectives, shards(): own = lax.all_to_all(ordered, (*SHARERS, SHARD_AXIS), 0, 0, tiled=True)  21.2 us
    all_to_all x1, starting transfers between devices, shards(): whole_head = lax.all_to_all(own_rows, SHARD_AXIS, 0, 0, tiled=True)  8.69 us
    all_to_all x1, waiting for transfers between devices, shards(): whole_head = lax.all_to_all(own_rows, SHARD_AXIS, 0, 0, tiled=True)  6.47 us
    ppermute x1, starting transfers between devices, shards(): other = lax.ppermute(own, 'core', [(0, 1), (1, 0)])  4.83 us
    pallas_call x1, Pallas kernels, shards(): pl.pallas_call(refit_kernel, out_shape=(jax.ShapeDtypeStruct(master.shape...  4.55 us
  transfers between devices with their start and end apart: 2, of which 2 were waited for; matrix products, arithmetic and copies ran while one was open for 0% of the time, Pallas kernels for 1%

profile of v10, /device:TPU:1, one launch (start us, length us, event | category | flops | bytes accessed | tf_op | source)
XLA Modules:
  0.0 95.6 jit_solution(12243123604349058635)
XLA Ops:
  0.6 1.6 %shard_map.85 = (bf16[16,16,512]{2,1,0:T(8,128)(2,1)}, f32[1,16,512]{2,1,0:T(8,128)}) custom-call(f32[1,16,512]{2,1,0:T(8,128)} %gradient.1, f32[1,16,512]{2,1,0:T(8,128)} %momentum.1), custom_call_target="tpu_custom_call" | custom-call | tf_op jit(solution)/shard_map/pallas_call | solution.py:188
  2.3 0.0 copy-start
  2.3 8.7 %all-to-all-start = ((bf16[16,16,512]{2,1,0:T(8,128)(2,1)}), bf16[16,16,512]{2,1,0:T(8,128)(2,1)S(1)}, u32[]{:S(2)}, u32[]{:S(2)}) async-start(bf16[16,16,512]{2,1,0:T(8,128)(2,1)} %get-tuple-element.9), calls=%async_computation | async-start | bytes 524288 | tf_op jit(solution)/shard_map/all_to_all | solution.py:203
  12.3 6.5 %all-to-all-done = bf16[16,16,512]{2,1,0:T(8,128)(2,1)S(1)} async-done(((bf16[16,16,512]{2,1,0:T(8,128)(2,1)}), bf16[16,16,512]{2,1,0:T(8,128)(2,1)S(1)}, u32[]{:S(2)}, u32[]{:S(2)}) %all-to-all-start) | async-done | bytes 262176 | tf_op jit(solution)/shard_map/all_to_all | solution.py:203
  18.8 0.0 copy-done
  18.8 4.5 %shard_map.86 = (f32[1,16,512]{2,1,0:T(8,128)S(1)}, bf16[64,8,128]{2,1,0:T(8,128)(2,1)S(1)}) custom-call(s32[1]{0:T(128)S(6)} %copy.11.count, f32[1]{0:T(128)S(6)} %copy.12.peak, bf16[256,512]{1,0:T(8,128)(2,1)S(1)} %bitcast.6, f32[1,16,512]{2,1,0:T(8,128)S(1)} %copy-done), custom_call_target="tpu_custom_call" | custom-call | tf_op jit(solution)/shard_map/pallas_call | solution.py:206
  23.3 0.0 copy-start.1
  23.3 43.2 %all_to_all.15.parts = bf16[64,8,128]{2,1,0:T(8,128)(2,1)S(1)} all-to-all(bf16[64,8,128]{2,1,0:T(8,128)(2,1)S(1)} %get-tuple-element.10), channel_id=1, replica_groups=mesh['xh'=2,'zh'=8,'zl'=2,'core'=2,'shard'=16] {'xh','zh','zl','core'}, dimensions={0} | all-to-all | bytes 262144 | tf_op jit(solution)/shard_map/all_to_all | solution.py:221
  66.6 0.0 copy-done.1
  66.6 0.6 shard_map.87
  67.2 21.2 %all_to_all.16 = bf16[64,4,8,128]{3,2,1,0:T(8,128)(2,1)S(1)} all-to-all(bf16[64,4,8,128]{3,2,1,0:T(8,128)(2,1)S(1)} %bitcast.5), channel_id=1, replica_groups=mesh['xh'=2,'zh'=8,'zl'=2,'core'=2,'shard'=16] {'xh','zl','shard'}, dimensions={0} | all-to-all | bytes 1048576 | tf_op jit(solution)/shard_map/all_to_all | solution.py:231
  88.4 4.8 %collective-permute-start = (bf16[2,2,16,4,8,128]{5,4,3,2,1,0:T(8,128)(2,1)S(1)}, bf16[2,2,16,4,8,128]{5,4,3,2,1,0:T(8,128)(2,1)S(1)}, u32[]{:S(2)}, u32[]{:S(2)}) collective-permute-start(bf16[2,2,16,4,8,128]{5,4,3,2,1,0:T(8,128)(2,1)S(1)} %bitcast.3), channel_id=1, source_target_pairs={{0,16},{16,0},{1,17},{17,1},{2,18},{18,2},{3,19},{19,3},{4,20},{20... | collective-permute-start | bytes 1572872 | tf_op jit(solution)/shard_map/ppermute | solution.py:233
  93.2 0.9 shard_map.88
  94.1 0.6 collective-permute-done.other
  94.7 0.9 shard_map.89
Async XLA Ops:
  2.3 16.5 %copy-start = (f32[1,16,512]{2,1,0:T(8,128)S(1)}, f32[1,16,512]{2,1,0:T(8,128)}, u32[]{:S(2)}) copy-start(f32[1,16,512]{2,1,0:T(8,128)} %master.1) | copy-start | bytes 98308
  2.3 16.5 %all-to-all-start = ((bf16[16,16,512]{2,1,0:T(8,128)(2,1)}), bf16[16,16,512]{2,1,0:T(8,128)(2,1)S(1)}, u32[]{:S(2)}, u32[]{:S(2)}) async-start(bf16[16,16,512]{2,1,0:T(8,128)(2,1)} %get-tuple-element.9), calls=%async_computation | async-start | bytes 524288 | tf_op jit(solution)/shard_map/all_to_all | solution.py:203
  23.3 43.3 %copy-start.1 = (s32[64]{0:T(128)S(1)}, s32[64]{0:T(128)}, u32[]{:S(2)}) copy-start(s32[64]{0:T(128)} %server_map.1) | copy-start | bytes 772
  88.4 6.4 %collective-permute-start = (bf16[2,2,16,4,8,128]{5,4,3,2,1,0:T(8,128)(2,1)S(1)}, bf16[2,2,16,4,8,128]{5,4,3,2,1,0:T(8,128)(2,1)S(1)}, u32[]{:S(2)}, u32[]{:S(2)}) collective-permute-start(bf16[2,2,16,4,8,128]{5,4,3,2,1,0:T(8,128)(2,1)S(1)} %bitcast.3), channel_id=1, source_target_pairs={{0,16},{16,0},{1,17},{17,1},{2,18},{18,2},{3,19},{19,3},{4,20},{20... | collective-permute-start | bytes 1572872 | tf_op jit(solution)/shard_map/ppermute | solution.py:233
